TPU v7x, 32 devices: a whole 2x2x4 slice. The times are simulated.
32 devices in a mesh: groups: 2 (over x), shot: 16 (over z, y, core).
Axes of the slice: x: 2, y: 2, z: 4, core: 2. Of those that a mesh axis runs over, the one named last changes fastest.
Arguments:
- velocity: float32 [2048, 16, 256], P(('groups', 'shot')), parts along dimension 0, may hold values from 0.2 to 0.4
- accumulated: float32 [2048, 16, 256], P(('groups', 'shot')), parts along dimension 0, may hold values from 0.1 to 1
- aperture_tiles: int32 [32, 32], P(('groups', 'shot')), parts along dimension 0, may hold values from 0 to 1023, as said below
- source_cell: int32 [32], P(('groups', 'shot')), parts along dimension 0, may hold values from 0 to 131071
- wavelet: float32 [32, 2], P(('groups', 'shot')), parts along dimension 0, may hold values from -6 to 6
- start_field: float32 [32, 2, 32, 32, 128], P(('groups', 'shot')), parts along dimension 0, may hold values from -6 to 6
- receiver_cells: int32 [32, 8192], P(('groups', 'shot')), parts along dimension 0, may hold values from 0 to 131071
- observed: float32 [32, 2, 8192], P(('groups', 'shot')), parts along dimension 0, may hold values from -6 to 6
Outputs:
- new_velocity: float32 [2048, 16, 256], P(('groups', 'shot')), parts along dimension 0
- new_accumulated: float32 [2048, 16, 256], P(('groups', 'shot')), parts along dimension 0
There are 2 independent parts, one for each index of `groups`. A program takes and returns all parts, laid end to end along the dimension named above; each array names one. Nothing has to cross between parts.
Inputs may be any that keep to these rules, and one draw needn't show every extreme that they name: `aperture_tiles`: each row names 32 distinct tile ids; the owner of a tile id is id // 64; a row names at most 4 tiles of one owner, and every row names exactly 4 tiles of some owner.
All inputs are finite; a program needn't handle non-finite values.
Results may differ from a plain program's by a relative error of at most 0.0001.
Values sent between devices are 32-bit elements; how exact they have to be, the bound alone decides.
No kernel may reach another device: no remote copies, remote signals or barrier semaphores. Data moves between devices by JAX's collectives and lax.ppermute only.
A program may use at most 192 MiB of HBM per device.

v0:
```python
import jax
import jax.numpy as jnp
from jax import lax
from jax.sharding import PartitionSpec as P

TS = 16
AX = 2
AY = 2
AZ = 8
STEPS = 2


stencil_weights = (-205.0 / 72.0, 8.0 / 5.0, -1.0 / 5.0, 8.0 / 315.0, -1.0 / 560.0)
step_rate = 0.02


def laplacian(wavefield):
    cells_first, cells_second, cells_third = wavefield.shape
    padded = jnp.pad(wavefield, 4)
    running = 3.0 * stencil_weights[0] * wavefield
    for offset in range(1, 5):
        weight = stencil_weights[offset]
        pair_first = (
            padded[4 + offset : 4 + offset + cells_first, 4 : 4 + cells_second, 4 : 4 + cells_third]
            + padded[
                4 - offset : 4 - offset + cells_first, 4 : 4 + cells_second, 4 : 4 + cells_third
            ]
        )
        pair_second = (
            padded[4 : 4 + cells_first, 4 + offset : 4 + offset + cells_second, 4 : 4 + cells_third]
            + padded[
                4 : 4 + cells_first, 4 - offset : 4 - offset + cells_second, 4 : 4 + cells_third
            ]
        )
        pair_third = (
            padded[4 : 4 + cells_first, 4 : 4 + cells_second, 4 + offset : 4 + offset + cells_third]
            + padded[
                4 : 4 + cells_first, 4 : 4 + cells_second, 4 - offset : 4 - offset + cells_third
            ]
        )
        running = running + weight * (pair_first + pair_second + pair_third)
    return running


def dense_misfit(courant, initial, source_index, wavelet_row, counts, observed_sums):
    squared = courant * courant
    previous = initial[0]
    current = initial[1]
    running = jnp.float32(0.0)
    for step_index in range(STEPS):
        future = 2.0 * current - previous + squared * laplacian(current)
        flat_field = future.reshape(-1).at[source_index].add(wavelet_row[step_index])
        running = running + jnp.sum(
            flat_field * (0.5 * counts * flat_field - observed_sums[step_index])
        )
        previous = current
        current = flat_field.reshape(future.shape)
    return running


def assemble(tile_block):
    blocks = tile_block.reshape(AX, AY, AZ, TS, TS, TS)
    return blocks.transpose(0, 3, 1, 4, 2, 5).reshape(AX * TS, AY * TS, AZ * TS)


def disassemble(volume):
    blocks = volume.reshape(AX, TS, AY, TS, AZ, TS).transpose(0, 2, 4, 1, 3, 5)
    return blocks.reshape(AX * AY * AZ, TS, TS * TS)


def shot_gradient(tile_block, source_index, wavelet_row, initial, receivers, recorded):
    volume = assemble(tile_block)
    cell_total = volume.shape[0] * volume.shape[1] * volume.shape[2]
    counts = jnp.zeros((cell_total,), jnp.float32).at[receivers].add(1.0)
    observed_sums = (
        jnp.zeros((recorded.shape[0], cell_total), jnp.float32).at[:, receivers].add(recorded)
    )
    derivative = jax.grad(dense_misfit)(
        volume, initial, source_index, wavelet_row, counts, observed_sums
    )
    return disassemble(derivative)


def slot_ranks(owners):
    entries = owners.shape[-1]
    earlier = jnp.arange(entries)[None, :] < jnp.arange(entries)[:, None]
    same_owner = owners[..., :, None] == owners[..., None, :]
    return jnp.sum(jnp.logical_and(same_owner, earlier), axis=-1)


def body(
    velocity,
    accumulated,
    aperture_tiles,
    source_cell,
    wavelet,
    start_field,
    receiver_cells,
    observed,
):
    devices = lax.axis_size("shot")
    own_index = lax.axis_index("shot")
    per_device = velocity.shape[0]
    capacity = max(2, 2 * (AX * AY * AZ) // devices)
    tile_ids = aperture_tiles[0]
    owners = tile_ids // per_device
    slot_index = owners * capacity + slot_ranks(owners)
    all_lists = lax.all_gather(aperture_tiles, "shot", axis=0, tiled=True)
    list_owners = all_lists // per_device
    matches = jnp.logical_and(
        list_owners[:, :, None] == own_index,
        slot_ranks(list_owners)[:, :, None] == jnp.arange(capacity, dtype=jnp.int32)[None, None, :],
    )
    wanted = jnp.max(jnp.where(matches, (all_lists % per_device)[:, :, None], -1), axis=1).reshape(
        -1
    )
    present = wanted >= 0
    safe_ids = jnp.where(present, wanted, 0)
    outgoing = velocity[safe_ids] * present[:, None, None].astype(jnp.float32)
    arrived = lax.all_to_all(outgoing, "shot", split_axis=0, concat_axis=0, tiled=True)
    tile_block = arrived[slot_index]
    gradient_tiles = shot_gradient(
        tile_block, source_cell[0], wavelet[0], start_field[0], receiver_cells[0], observed[0]
    )
    outgoing_gradient = (
        jnp.zeros((devices * capacity,) + velocity.shape[1:], jnp.float32)
        .at[slot_index]
        .set(gradient_tiles)
    )
    returned = lax.all_to_all(outgoing_gradient, "shot", split_axis=0, concat_axis=0, tiled=True)
    pooled = jnp.zeros(velocity.shape, jnp.float32).at[safe_ids].add(returned)
    new_accumulated = accumulated + pooled * pooled
    new_velocity = velocity - step_rate * pooled / jnp.sqrt(new_accumulated)
    return (new_velocity, new_accumulated)


def solution(mesh):
    return jax.shard_map(
        body,
        mesh=mesh,
        in_specs=(
            P(("groups", "shot"), None, None),
            P(("groups", "shot"), None, None),
            P(("groups", "shot"), None),
            P(("groups", "shot")),
            P(("groups", "shot"), None),
            P(("groups", "shot"), None, None, None, None),
            P(("groups", "shot"), None),
            P(("groups", "shot"), None, None),
        ),
        out_specs=(P(("groups", "shot"), None, None), P(("groups", "shot"), None, None)),
        check_vma=False,
    )
```

profile of v0, /device:TPU:1, one launch (start us, length us, event | category | flops | bytes accessed | tf_op | source)
XLA Modules:
  0.0 365.1 jit_solution(10400257393337121836)
XLA Ops:
  0.6 23.0 %all-gather = s32[16,1,32]{2,1,0:T(1,128)S(1)} all-gather(s32[1,1,32]{2,1,0:T(1,128)} %bitcast.92), channel_id=1, replica_groups=mesh['groups'=2,'shot'=16] {'shot'}, dimensions={0}, use_global_device_ids=true | all-gather | bytes 2176 | tf_op jit(solution)/shard_map/all_gather | solution.py:108
  24.7 1.8 gather_fusion
  26.6 1.1 broadcast_multiply_fusion
  27.7 3.6 all-to-all-start
  31.7 2.7 copy.26
  34.3 5.9 %sort = (s32[8192]{0:T(1024)S(1)}, s32[8192]{0:T(1024)S(1)}) sort(s32[8192]{0:T(1024)S(1)} %bitcast.87, s32[8192]{0:T(1024)S(1)} %iota.23), dimensions={0}, to_apply=%compare | sort | flops 106496 | bytes 131072 | tf_op jit(solution)/shard_map/scatter-add | solution.py:76
  40.3 0.8 slice_bitcast_fusion
  41.8 0.6 fusion.78
  42.4 43.5 %scatter_custom_fusion = f32[131072]{0:T(1024)S(1)} fusion(s32[8192]{0:T(1024)S(1)} %bitcast.88, f32[8192]{0:T(1024)S(1)} %broadcast.302, f32[]{:T(128)} %constant.98.clone.1), kind=kCustom, calls=%fused_computation.142 | custom fusion | flops 8192 | bytes 524292 | tf_op jit(solution)/shard_map/scatter-add | solution.py:74
  85.9 121.7 %scatter_custom_fusion.1 = f32[2,131072]{0,1:T(8,128)} fusion(s32[8192]{0:T(1024)S(1)} %get-tuple-element.26, f32[]{:T(128)} %constant.98.clone.1, f32[8192,2]{1,0:T(8,128)} %copy.26, s32[8192]{0:T(1024)S(1)} %broadcast_clamp_fusion), kind=kCustom, calls=%fused_computation.9 | custom fusion | flops 16384 | bytes 1049088 | tf_op jit(solution)/shard_map/scatter-add | solution.py:76
  207.6 66.5 %slice_reduce_fusion = (f32[131072]{0:T(1024)}, f32[131072]{0:T(1024)}) fusion(f32[2,131072]{0,1:T(8,128)} %scatter_custom_fusion.1), kind=kLoop, calls=%fused_computation.7 | loop fusion | bytes 2097152 | tf_op jit(solution)/shard_map/jvp()/slice | solution.py:54
  274.1 1.4 gather_fusion.1
  275.5 1.2 fusion.77
  276.7 2.6 reshape.299
  279.3 6.6 %copy.33 = f32[2,2,8,16,16,16]{5,2,4,1,3,0:T(8,128)} copy(f32[2,2,8,16,16,16]{5,4,3,2,1,0:T(8,128)} %reshape.299) | data formatting | bytes 1048576 | tf_op jit(solution)/shard_map/transpose(jvp())/mul | solution.py:46
  285.9 3.2 reshape.297
  289.1 2.6 reshape.298
  291.7 6.6 %copy.32 = f32[2,2,8,16,16,16]{5,2,4,1,3,0:T(8,128)} copy(f32[2,2,8,16,16,16]{5,4,3,2,1,0:T(8,128)} %reshape.298) | data formatting | bytes 1048576 | tf_op jit(solution)/shard_map/jvp()/mul | solution.py:46
  298.3 3.3 reshape.296
  301.6 1.2 fusion.64
  302.8 1.0 fusion.70
  303.8 1.2 multiply_add_fusion.1
  304.9 0.8 fusion.71
  306.1 7.4 %pad_add_fusion = f32[40,40,136]{2,1,0:T(8,128)S(1)} fusion(f32[32,32,128]{2,1,0:T(8,128)S(1)} %get-tuple-element.43, f32[32,32,128]{2,1,0:T(8,128)S(1)} %get-tuple-element.42, f32[32,32,128]{2,1,0:T(8,128)S(1)} %get-tuple-element.32), kind=kLoop, calls=%fused_computation.63 | loop fusion | flops 3699200 | bytes 2443264 | tf_op jit(solution)/shard_map/transpose(jvp())/add_any | solution.py:24
  314.1 0.5 copy-done.2
  315.0 2.5 reshape.293
  317.6 4.9 %copy.31 = f32[2,16,2,16,8,16]{5,3,1,4,2,0:T(8,128)} copy(f32[2,16,2,16,8,16]{5,4,3,2,1,0:T(8,128)} %reshape.293) | data formatting | bytes 1048576 | tf_op jit(solution)/shard_map/reshape | solution.py:67
  322.5 3.5 reshape.336
  326.1 1.5 scatter_fusion
  327.6 31.1 %all_to_all.10 = f32[64,16,256]{2,1,0:T(8,128)S(1)} all-to-all(f32[64,16,256]{2,1,0:T(8,128)S(1)} %scatter_fusion), channel_id=1, replica_groups=mesh['groups'=2,'shot'=16] {'shot'}, dimensions={0} | all-to-all | bytes 2097152 | tf_op jit(solution)/shard_map/all_to_all | solution.py:130
  358.8 3.2 scatter_fusion.1
  362.0 2.9 multiply_subtract_fusion
  (47 shorter events, 2.9 us)
Async XLA Ops:
  26.5 4.8 %copy-start.8 = (s32[1,32]{1,0:T(1,128)S(1)}, s32[1,32]{1,0:T(1,128)}, u32[]{:S(2)}) copy-start(s32[1,32]{1,0:T(1,128)} %param.14) | copy-start | bytes 388
  26.6 5.0 %copy-start.6 = (s32[1,8192]{1,0:T(1,128)S(1)}, s32[1,8192]{1,0:T(1,128)}, u32[]{:S(2)}) copy-start(s32[1,8192]{1,0:T(1,128)} %param.18) | copy-start | bytes 98308
  26.6 5.1 %copy-start.5 = (f32[1,2,8192]{2,1,0:T(2,128)S(1)}, f32[1,2,8192]{2,1,0:T(2,128)}, u32[]{:S(2)}) copy-start(f32[1,2,8192]{2,1,0:T(2,128)} %param.19) | copy-start | bytes 196612
  27.7 246.4 %all-to-all-start = ((f32[64,16,256]{2,1,0:T(8,128)}), f32[64,16,256]{2,1,0:T(8,128)S(1)}, u32[]{:S(2)}, u32[]{:S(2)}) async-start(f32[64,16,256]{2,1,0:T(8,128)} %broadcast_multiply_fusion), calls=%async_computation | async-start | bytes 2097152 | tf_op jit(solution)/shard_map/all_to_all | solution.py:120
  31.6 8.7 %copy-start = (f32[1,2,32,32,128]{4,3,2,1,0:T(8,128)S(1)}, f32[1,2,32,32,128]{4,3,2,1,0:T(8,128)}, u32[]{:S(2)}) copy-start(f32[1,2,32,32,128]{4,3,2,1,0:T(8,128)} %param.17) | copy-start | bytes 3145732
  31.6 10.1 %copy-start.7 = (f32[1,2]{1,0:T(1,128)S(1)}, f32[1,2]{1,0:T(1,128)}, u32[]{:S(2)}) copy-start(f32[1,2]{1,0:T(1,128)} %param.16) | copy-start | bytes 28
  298.3 3.3 copy-start.4
  302.8 3.0 copy-start.3
  313.6 1.0 copy-start.2
  358.8 3.2 copy-start.1
where the time goes:
time: 371 us; the launch traced here: 365 us
  other arithmetic  193 us (52%)
  local copies, waits for them, and re-layouts  112 us (30%)
  blocking collectives  54.1 us (15%)
    scatter-add x3, other arithmetic, shot_gradient(): jnp.zeros((recorded.shape[0], cell_total), jnp.float32).at[:, receivers]  128 us
    slice x1, local copies, waits for them, and re-layouts, dense_misfit(): observed_sums[step_index]  66.5 us
    scatter-add x1, other arithmetic, shot_gradient(): counts = jnp.zeros((cell_total,), jnp.float32).at[receivers].add(1.0)  43.5 us
    all_to_all x1, blocking collectives, body(): lax.all_to_all(outgoing_gradient, 'shot', split_axis=0, concat_axis=0, ti...  31.1 us
    mul x6, local copies, waits for them, and re-layouts, dense_misfit(): squared = courant * courant  24.9 us
    all_gather x1, blocking collectives, body(): all_lists = lax.all_gather(aperture_tiles, 'shot', axis=0, tiled=True)  23 us
    reshape x2, local copies, waits for them, and re-layouts, disassemble(): blocks = volume.reshape(AX, TS, AY, TS, AZ, TS).transpose(0, 2, 4, 1, 3, 5)  7.44 us
  transfers between devices with their start and end apart: 1, of which 0 were waited for; matrix products, arithmetic and copies ran while one was open for 66% of the time, Pallas kernels for 0%

commit v1 on v0

v1 whole, which is shorter than its diff:
```python
import functools

import jax
import jax.numpy as jnp
import numpy as np
from jax import lax
from jax.experimental import pallas as pl
from jax.experimental.pallas import tpu as pltpu
from jax.sharding import PartitionSpec as P

TS = 16
AX = 2
AY = 2
AZ = 8
BX = AX * TS
BY = AY * TS
APT = AX * AY * AZ
ROWS = BX * AZ
LANES = BY * TS
HALF = TS * TS
PAD = 4 * AZ
CHUNK = 512

scaled_weights = (-14350.0, 8064.0, -1008.0, 128.0, -9.0)
weight_scale = 1.0 / 5040.0
step_rate = 0.02


def stencil_matrices():
    lane = np.arange(LANES)
    y, l = lane // TS, lane % TS
    same = np.zeros((LANES, LANES), np.float32)
    cross = np.zeros((LANES, LANES), np.float32)
    for offset in range(1, 5):
        w = scaled_weights[offset]
        dy = np.abs(y[:, None] - y[None, :])
        dl = np.abs(l[:, None] - l[None, :])
        same += w * ((dl == 0) & (dy == offset))
        same += w * ((dy == 0) & (dl == offset))
        cross += w * ((dy == 0) & (dl == TS - offset))
    return same, cross[:HALF, :HALF]


def split(value):
    high = value.astype(jnp.bfloat16)
    rest = value - high.astype(jnp.float32)
    middle = rest.astype(jnp.bfloat16)
    low = (rest - middle.astype(jnp.float32)).astype(jnp.bfloat16)
    return high, middle, low


def stencil_products(field, parts, near, far, same_ref, cross_ref):
    for row in range(0, ROWS, 16):
        pieces = split(field[PAD + row : PAD + row + 16, :])
        for p in range(3):
            parts[p, row : row + 16, :] = pieces[p]
    same = same_ref[...]
    cross = cross_ref[...]
    dot = functools.partial(jnp.dot, preferred_element_type=jnp.float32)
    near[...] = dot(parts[0], same) + dot(parts[1], same) + dot(parts[2], same)
    for side in range(0, LANES, HALF):
        cols = slice(side, side + HALF)
        far[:, cols] = (
            dot(parts[0, :, cols], cross) + dot(parts[1, :, cols], cross) + dot(parts[2, :, cols], cross)
        )


def laplacian_rows(field, near, far, row, upper, keep):
    at = PAD + row
    total = near[row : row + AZ, :] + 3.0 * scaled_weights[0] * field[at : at + AZ, :]
    for offset in range(1, 5):
        above = field[at + offset * AZ : at + offset * AZ + AZ, :]
        below = field[at - offset * AZ : at - offset * AZ + AZ, :]
        total = total + scaled_weights[offset] * (above + below)
    other = far[row : row + AZ, :]
    moved = jnp.where(upper, pltpu.roll(other, AZ - 1, 0), pltpu.roll(other, 1, 0))
    return weight_scale * (total + jnp.where(keep, moved, 0.0))


def far_masks():
    lane = lax.broadcasted_iota(jnp.int32, (AZ, LANES), 1) % TS
    row = lax.broadcasted_iota(jnp.int32, (AZ, LANES), 0)
    upper = lane >= TS // 2
    keep = row != jnp.where(upper, AZ - 1, 0)
    return upper, keep


def clear_pads(field):
    zero = jnp.zeros((PAD, LANES), jnp.float32)
    field[:PAD, :] = zero
    field[PAD + ROWS :, :] = zero


def request_kernel(capacity, per_device, ids, table, slots, counts):
    devices = table.shape[0]
    for owner in range(devices):
        counts[owner] = 0
    owner_of = lax.broadcasted_iota(jnp.int32, table.shape, 0)
    rank_of = lax.broadcasted_iota(jnp.int32, table.shape, 1)
    position = owner_of * capacity + jnp.where(rank_of < capacity, rank_of, -devices * capacity)
    found = jnp.full(table.shape, -1, jnp.int32)
    for k in range(APT):
        tile = ids[0, k]
        owner = tile // per_device
        rank = counts[owner]
        counts[owner] = rank + 1
        slot = owner * capacity + rank
        slots[0, k] = slot
        found = jnp.where(position == slot, tile - owner * per_device, found)
    table[...] = found


def gather_kernel(capacity, wanted, velocity, outgoing):
    devices = wanted.shape[0]

    def step(shot, carry):
        for rank in range(capacity):
            tile = jnp.maximum(wanted[shot, rank], 0)
            outgoing[shot * capacity + rank] = velocity[tile]
        return carry

    lax.fori_loop(0, devices, step, 0, unroll=4)


def prepare_kernel(source, wavelet, start, same_ref, cross_ref, lap0, base1, base2, field, parts, near, far):
    clear_pads(field)
    cell = source[0]
    sx, sy, sz = cell // (BY * AZ * TS), (cell // (AZ * TS)) % BY, cell % (AZ * TS)
    source_row = sx * AZ + sz // TS
    source_lane = sy * TS + sz % TS
    lane = lax.broadcasted_iota(jnp.int32, (8, 128), 1)
    sub = lax.broadcasted_iota(jnp.int32, (8, 128), 0)
    wide_lane = lax.broadcasted_iota(jnp.int32, (AZ, LANES), 1)
    wide_row = lax.broadcasted_iota(jnp.int32, (AZ, LANES), 0)

    def turn(block):
        for bit in (1, 2, 4):
            sub_bit = sub & bit
            lane_bit = (lane // TS) & bit
            up = pltpu.roll(pltpu.roll(block, 8 - bit, 0), bit * TS, 1)
            down = pltpu.roll(pltpu.roll(block, bit, 0), 128 - bit * TS, 1)
            block = jnp.where(sub_bit == lane_bit, block, jnp.where(lane_bit != 0, up, down))
        return block

    for x in range(BX):
        hit = (wide_row == source_row - x * AZ) & (wide_lane == source_lane)
        previous = jnp.concatenate([turn(start[0, x, y : y + 8, :]) for y in range(0, BY, 8)], axis=1)
        current = jnp.concatenate([turn(start[1, x, y : y + 8, :]) for y in range(0, BY, 8)], axis=1)
        rows = slice(x * AZ, x * AZ + AZ)
        field[PAD + x * AZ : PAD + x * AZ + AZ, :] = current
        base1[rows, :] = 2.0 * current - previous + jnp.where(hit, wavelet[0, 0], 0.0)
        base2[rows, :] = jnp.where(hit, wavelet[0, 1], 0.0) - current
    stencil_products(field, parts, near, far, same_ref, cross_ref)
    upper, keep = far_masks()
    for x in range(BX):
        lap0[x * AZ : x * AZ + AZ, :] = laplacian_rows(field, near, far, x * AZ, upper, keep)


def receivers_kernel(cells, recorded, counts, sums0, sums1, left, right):
    step = pl.program_id(0)
    here = pl.ds(pl.multiple_of(step * CHUNK, CHUNK), CHUNK)
    cell = cells[:, here]
    x, y, z = cell // (BY * AZ * TS), (cell // (AZ * TS)) % BY, cell % (AZ * TS)
    row = x * AZ + z // TS
    lane = y * TS + z % TS
    row_hot = jnp.where(lax.broadcasted_iota(jnp.int32, (ROWS, CHUNK), 0) == row, 1.0, 0.0).astype(jnp.bfloat16)
    right[...] = jnp.where(lax.broadcasted_iota(jnp.int32, (LANES, CHUNK), 0) == lane, 1.0, 0.0).astype(jnp.bfloat16)
    left[:ROWS, :] = row_hot
    for n in range(2):
        pieces = split(jnp.broadcast_to(recorded[n : n + 1, here], (16, CHUNK)))
        for p in range(3):
            at = (1 + 3 * n + p) * ROWS
            left[at : at + ROWS, :] = (row_hot.reshape(ROWS // 16, 16, CHUNK) * pieces[p][None]).reshape(ROWS, CHUNK)

    @pl.when(step == 0)
    def _():
        for ref in (counts, sums0, sums1):
            ref[...] = jnp.zeros_like(ref)

    def hits(part):
        return lax.dot_general(
            left[part * ROWS : (part + 1) * ROWS, :], right[...], (((1,), (1,)), ((), ())),
            preferred_element_type=jnp.float32,
        )

    counts[...] += hits(0)
    sums0[...] += hits(1) + hits(2) + hits(3)
    sums1[...] += hits(4) + hits(5) + hits(6)


def joined(ref, rows):
    return jnp.concatenate([ref[part, rows, :] for part in range(4)], axis=1)


def gradient_kernel(
    slots, arrived, lap0, base1, base2, counts, sums0, sums1, same_ref, cross_ref,
    outgoing, courant, field1, field2, partial, parts, near, far,
):
    for k in range(APT):
        kx, ky, kz = k // (AY * AZ), (k // AZ) % AY, k % AZ
        tile = arrived[slots[0, k]]
        for part in range(2):
            courant[2 * ky + part, pl.ds(kx * TS * AZ + kz, TS, AZ), :] = tile[:, part * 128 : part * 128 + 128]
    clear_pads(field1)
    clear_pads(field2)
    for x in range(BX):
        rows = slice(x * AZ, x * AZ + AZ)
        speed = joined(courant, rows)
        field1[PAD + x * AZ : PAD + x * AZ + AZ, :] = base1[rows, :] + speed * speed * lap0[rows, :]
    stencil_products(field1, parts, near, far, same_ref, cross_ref)
    upper, keep = far_masks()
    for x in range(BX):
        rows = slice(x * AZ, x * AZ + AZ)
        own = slice(PAD + x * AZ, PAD + x * AZ + AZ)
        speed = joined(courant, rows)
        squared = speed * speed
        bent = laplacian_rows(field1, near, far, x * AZ, upper, keep)
        after = 2.0 * field1[own, :] + base2[rows, :] + squared * bent
        miss2 = counts[rows, :] * after - sums1[rows, :]
        field2[own, :] = squared * miss2
        base = counts[rows, :] * field1[own, :] - sums0[rows, :] + 2.0 * miss2
        partial[rows, :] = miss2 * bent + base * lap0[rows, :]
    stencil_products(field2, parts, near, far, same_ref, cross_ref)
    for x in range(BX):
        rows = slice(x * AZ, x * AZ + AZ)
        bent = laplacian_rows(field2, near, far, x * AZ, upper, keep)
        result = 2.0 * joined(courant, rows) * (partial[rows, :] + bent * lap0[rows, :])
        for part in range(4):
            courant[part, rows, :] = result[:, part * 128 : part * 128 + 128]
    for k in range(APT):
        kx, ky, kz = k // (AY * AZ), (k // AZ) % AY, k % AZ
        for part in range(2):
            outgoing[slots[0, k], :, part * 128 : part * 128 + 128] = courant[
                2 * ky + part, pl.ds(kx * TS * AZ + kz, TS, AZ), :
            ]


def update_kernel(capacity, wanted, returned, velocity, accumulated, new_velocity, new_accumulated, pooled):
    devices = wanted.shape[0]
    block = velocity.shape[0]
    tiles = pooled.shape[0] - 1
    step = pl.program_id(0)

    @pl.when(step == 0)
    def _():
        for tile in range(tiles):
            pooled[tile] = jnp.zeros(pooled.shape[1:], jnp.float32)

        def add(shot, carry):
            for rank in range(capacity):
                tile = wanted[shot, rank]
                tile = jnp.where(tile < 0, tiles, tile)
                pooled[tile] += returned[shot * capacity + rank]
            return carry

        lax.fori_loop(0, devices, add, 0)

    gradient = pooled[pl.ds(step * block, block)]
    total = accumulated[...] + gradient * gradient
    new_accumulated[...] = total
    new_velocity[...] = velocity[...] - step_rate * gradient / jnp.sqrt(total)


VMEM = pl.BlockSpec(memory_space=pltpu.VMEM)
SMEM = pl.BlockSpec(memory_space=pltpu.SMEM)
MIB = 2**20


def params(mib):
    return pltpu.CompilerParams(vmem_limit_bytes=mib * MIB)


def f32(*shape):
    return jax.ShapeDtypeStruct(shape, jnp.float32)


def body(velocity, accumulated, aperture_tiles, source_cell, wavelet, start_field, receiver_cells, observed):
    devices = lax.axis_size("shot")
    per_device = velocity.shape[0]
    capacity = max(2, 2 * APT // devices)
    same, cross = stencil_matrices()
    same = jnp.asarray(same, jnp.bfloat16)
    cross = jnp.asarray(cross, jnp.bfloat16)

    table, slots = pl.pallas_call(
        functools.partial(request_kernel, capacity, per_device),
        out_shape=(
            jax.ShapeDtypeStruct((devices, 128), jnp.int32),
            jax.ShapeDtypeStruct((1, APT), jnp.int32),
        ),
        in_specs=[SMEM],
        out_specs=(VMEM, SMEM),
        scratch_shapes=[pltpu.SMEM((devices,), jnp.int32)],
        name="requests",
    )(aperture_tiles)
    wanted = lax.all_to_all(table, "shot", split_axis=0, concat_axis=0, tiled=True)

    fields = (ROWS, LANES)
    padded = pltpu.VMEM((ROWS + 2 * PAD, LANES), jnp.float32)
    whole = pltpu.VMEM(fields, jnp.float32)
    pieces = pltpu.VMEM((3,) + fields, jnp.bfloat16)
    lap0, base1, base2 = pl.pallas_call(
        prepare_kernel,
        out_shape=(f32(*fields),) * 3,
        in_specs=[SMEM, SMEM, VMEM, VMEM, VMEM],
        out_specs=(VMEM,) * 3,
        scratch_shapes=[padded, pieces, whole, whole],
        compiler_params=params(16),
        cost_estimate=pl.CostEstimate(flops=10**9, bytes_accessed=4 * MIB, transcendentals=0),
        name="prepare",
    )(source_cell, wavelet, start_field[0], same, cross)

    outgoing = pl.pallas_call(
        functools.partial(gather_kernel, capacity),
        out_shape=f32(devices * capacity, *velocity.shape[1:]),
        in_specs=[SMEM, VMEM],
        out_specs=VMEM,
        compiler_params=params(16),
        name="gather",
    )(wanted, velocity)
    arrived = lax.all_to_all(outgoing, "shot", split_axis=0, concat_axis=0, tiled=True)

    receivers = receiver_cells.shape[1]
    counts, sums0, sums1 = pl.pallas_call(
        receivers_kernel,
        out_shape=(f32(*fields),) * 3,
        grid=(receivers // CHUNK,),
        in_specs=[VMEM, VMEM],
        out_specs=(pl.BlockSpec(fields, lambda i: (0, 0)),) * 3,
        scratch_shapes=[
            pltpu.VMEM((7 * ROWS, CHUNK), jnp.bfloat16),
            pltpu.VMEM((LANES, CHUNK), jnp.bfloat16),
        ],
        compiler_params=params(24),
        cost_estimate=pl.CostEstimate(flops=15 * 10**9, bytes_accessed=2 * MIB, transcendentals=0),
        name="receivers",
    )(receiver_cells, observed[0])

    outgoing_gradient = pl.pallas_call(
        gradient_kernel,
        out_shape=f32(devices * capacity, *velocity.shape[1:]),
        in_specs=[SMEM] + [VMEM] * 9,
        out_specs=VMEM,
        scratch_shapes=[pltpu.VMEM((4, ROWS, 128), jnp.float32), padded, padded, whole, pieces, whole, whole],
        compiler_params=params(24),
        name="gradient",
    )(slots, arrived, lap0, base1, base2, counts, sums0, sums1, same, cross)
    returned = lax.all_to_all(outgoing_gradient, "shot", split_axis=0, concat_axis=0, tiled=True)

    tile = velocity.shape[1:]
    block = 8
    by_block = pl.BlockSpec((block,) + tile, lambda i: (i, 0, 0))
    return pl.pallas_call(
        functools.partial(update_kernel, capacity),
        out_shape=(f32(*velocity.shape),) * 2,
        grid=(per_device // block,),
        in_specs=[SMEM, VMEM, by_block, by_block],
        out_specs=(by_block,) * 2,
        scratch_shapes=[pltpu.VMEM((per_device + 1,) + tile, jnp.float32)],
        compiler_params=params(16),
        name="update",
    )(wanted, returned, velocity, accumulated)


def solution(mesh):
    split_shots = ("groups", "shot")
    return jax.shard_map(
        body,
        mesh=mesh,
        in_specs=(
            P(split_shots, None, None),
            P(split_shots, None, None),
            P(split_shots, None),
            P(split_shots),
            P(split_shots, None),
            P(split_shots, None, None, None, None),
            P(split_shots, None),
            P(split_shots, None, None),
        ),
        out_specs=(P(split_shots, None, None), P(split_shots, None, None)),
        check_vma=False,
    )
```

time: 371 us -> 114 us (0.31); the launches traced: 365 us -> 114 us
  other arithmetic: 193 us -> 0 us
  local copies, waits for them, and re-layouts: 112 us -> 9.27 us
  Pallas kernels: 0 us -> 54.5 us
  blocking collectives: 54.1 us -> 44.3 us
    scatter-add x7 -> x0, other arithmetic: 176 us -> none  [the longest x3 128 us: shot_gradient(): jnp.zeros((recorded.shape[0], cell_total), jnp.float32).at[:, receivers]]
    slice x2 -> x0, local copies, waits for them, and re-layouts: 67.1 us -> none  [the longest x1 66.5 us: dense_misfit(): observed_sums[step_index]]
    pallas_call x0 -> x6, Pallas kernels: none -> 54.5 us  [the longest x1 23.5 us: body(): pl.pallas_call(receivers_kernel, out_shape=(f32(*fields),) * 3, grid=(rec...]
    mul x6 -> x0, local copies, waits for them, and re-layouts: 24.9 us -> none  [dense_misfit(): squared = courant * courant]
    all_gather x1 -> x0, blocking collectives: 23 us -> none  [body(): all_lists = lax.all_gather(aperture_tiles, 'shot', axis=0, tiled=True)]
    all_to_all x0 -> x1, blocking collectives: none -> 13.1 us  [body(): lax.all_to_all(table, 'shot', split_axis=0, concat_axis=0, tiled=True)]
    reshape x4 -> x0, local copies, waits for them, and re-layouts: 11 us -> none  [the longest x2 7.44 us: disassemble(): blocks = volume.reshape(AX, TS, AY, TS, AZ, TS).transpose(0, 2, 4, 1, 3, 5)]
    unnamed x18 -> x32, local copies, waits for them, and re-layouts: 0.57 us -> 9.27 us
  transfers between devices with their start and end apart: 1 -> 1, of which waited for: 0 -> 0; matrix products, arithmetic and copies ran while one was open for 66% -> 0% of each run, Pallas kernels for 0% -> 39%
where the time goes in v1:
time: 114 us
  Pallas kernels  54.5 us (48%)
  blocking collectives  44.3 us (39%)
  local copies, waits for them, and re-layouts  9.27 us (8%)
  starting transfers between devices  4.3 us (4%)
  between operations  1.39 us (1%)
    all_to_all x1, blocking collectives, body(): lax.all_to_all(outgoing_gradient, 'shot', split_axis=0, concat_axis=0, ti...  31.2 us
    pallas_call x1, Pallas kernels, body(): pl.pallas_call(receivers_kernel, out_shape=(f32(*fields),) * 3, grid=(rec...  23.5 us
    pallas_call x1, Pallas kernels, body(): pl.pallas_call(prepare_kernel, out_shape=(f32(*fields),) * 3, in_specs=[S...  20.7 us
    all_to_all x1, blocking collectives, body(): lax.all_to_all(table, 'shot', split_axis=0, concat_axis=0, tiled=True)  13.1 us
    unnamed x32, local copies, waits for them, and re-layouts  9.27 us
    all_to_all x1, starting transfers between devices, body(): lax.all_to_all(outgoing, 'shot', split_axis=0, concat_axis=0, tiled=True)  4.3 us
    pallas_call x1, Pallas kernels, body(): pl.pallas_call(functools.partial(update_kernel, capacity), out_shape=(f32...  4.11 us
    pallas_call x1, Pallas kernels, body(): pl.pallas_call(gradient_kernel, out_shape=f32(devices * capacity, *veloci...  2.88 us
  transfers between devices with their start and end apart: 1, of which 0 were waited for; matrix products, arithmetic and copies ran while one was open for 0% of the time, Pallas kernels for 39%

profile of v1, /device:TPU:1, one launch (start us, length us, event | category | flops | bytes accessed | tf_op | source)
XLA Modules:
  0.0 113.7 jit_solution(13426275312382176213)
XLA Ops:
  0.6 1.5 %requests.1 = (s32[16,128]{1,0:T(8,128)}, s32[1,32]{1,0:T(1,128)}) custom-call(s32[1,32]{1,0:T(1,128)} %ids.1), custom_call_target="tpu_custom_call" | custom-call | tf_op jit(solution)/shard_map/requests/pallas_call | solution.py:285
  2.1 13.1 %all_to_all.21 = s32[16,1,128]{2,1,0:T(1,128)S(1)} all-to-all(s32[16,1,128]{2,1,0:T(1,128)} %bitcast.10), channel_id=1, replica_groups=mesh['groups'=2,'shot'=16] {'shot'}, dimensions={0} | all-to-all | bytes 16384 | tf_op jit(solution)/shard_map/all_to_all | solution.py:296
  15.2 0.0 copy-start
  15.2 1.2 %copy-done = f32[64,16,256]{2,1,0:T(8,128)S(1)} copy-done((f32[64,16,256]{2,1,0:T(8,128)S(1)}, f32[64,16,256]{2,1,0:T(8,128)}, u32[]{:S(2)}) %copy-start) | copy-done | bytes 1048600
  16.4 1.8 %gather.1 = f32[64,16,256]{2,1,0:T(8,128)} custom-call(s32[16,128]{1,0:T(8,128)S(1)} %bitcast.6, f32[64,16,256]{2,1,0:T(8,128)S(1)} %copy-done), custom_call_target="tpu_custom_call" | custom-call | tf_op jit(solution)/shard_map/gather/pallas_call | solution.py:313
  18.2 0.0 copy-start.3
  18.2 4.3 %all-to-all-start.1 = ((f32[64,16,256]{2,1,0:T(8,128)}), f32[64,16,256]{2,1,0:T(8,128)S(1)}, u32[]{:S(2)}, u32[]{:S(2)}) async-start(f32[64,16,256]{2,1,0:T(8,128)} %gather.1), calls=%async_computation.1 | async-start | bytes 2097152 | tf_op jit(solution)/shard_map/all_to_all | solution.py:321
  23.1 0.0 copy-start.15
  23.2 0.0 copy-done.3
  23.2 0.0 copy-done.10
  23.2 0.6 copy-done.15
  23.8 1.2 %copy-done.12 = f32[1,2,32,32,128]{4,3,2,1,0:T(8,128)S(1)} copy-done((f32[1,2,32,32,128]{4,3,2,1,0:T(8,128)S(1)}, f32[1,2,32,32,128]{4,3,2,1,0:T(8,128)}, u32[]{:S(2)}) %copy-start.12) | copy-done | bytes 1048600
  25.0 20.7 %prepare.1 = (f32[256,512]{1,0:T(8,128)S(1)}, f32[256,512]{1,0:T(8,128)S(1)}, f32[256,512]{1,0:T(8,128)S(1)}) custom-call(s32[1]{0:T(128)S(6)} %copy.13.source, f32[1,2]{1,0:T(1,128)S(1)} %copy-done.15, f32[2,32,32,128]{3,2,1,0:T(8,128)S(1)} %bitcast.8, bf16[512,512]{1,0:T(8,128)(2,1)S(1)} %copy-done.3, bf16[256,256]{1,0:T(8,128)(2,1)S(1)} %copy-done.10), custom_call_target="tpu_custom_call" | custom-call | flops 1000000000 | bytes 4194304 | tf_op jit(solution)/shard_map/prepare/pallas_call | solution.py:302
  45.7 0.0 copy-done.13
  45.7 0.0 copy-done.14
  45.7 23.5 %receivers.1 = (f32[256,512]{1,0:T(8,128)S(1)}, f32[256,512]{1,0:T(8,128)S(1)}, f32[256,512]{1,0:T(8,128)S(1)}) custom-call(s32[1,8192]{1,0:T(1,128)S(1)} %copy-done.14, f32[2,8192]{1,0:T(2,128)S(1)} %bitcast.9), custom_call_target="tpu_custom_call" | custom-call | flops 15000000512 | bytes 2097152 | tf_op jit(solution)/shard_map/receivers/pallas_call | solution.py:324
  69.3 0.0 copy-start.4
  69.3 0.8 copy-done.4
  70.1 0.8 copy-done.6
  70.9 0.8 copy-done.8
  71.7 0.0 all-to-all-done.1.arrived
  71.7 0.7 copy-done.11
  72.3 1.0 copy-done.5
  73.4 1.0 copy-done.7
  74.4 1.0 copy-done.9
  75.5 2.9 %gradient.1 = f32[64,16,256]{2,1,0:T(8,128)S(1)} custom-call(s32[1,32]{1,0:T(1,128)S(1)} %copy-done.11, f32[64,16,256]{2,1,0:T(8,128)S(1)} %all-to-all-done.1.arrived, f32[256,512]{1,0:T(8,128)S(1)} %get-tuple-element.12.lap0, f32[256,512]{1,0:T(8,128)S(1)} %get-tuple-element.13.base1, f32[256,512]{1,0:T(8,128)S(1)} %get-tuple-element.14.base2, ...), custom_call_target="tpu_custom_call" | custom-call | tf_op jit(solution)/shard_map/gradient/pallas_call | solution.py:339
  78.4 0.0 copy-start.1
  78.4 0.0 copy-start.2
  78.4 31.2 %all_to_all.22.returned = f32[64,16,256]{2,1,0:T(8,128)S(1)} all-to-all(f32[64,16,256]{2,1,0:T(8,128)S(1)} %gradient.1), channel_id=1, replica_groups=mesh['groups'=2,'shot'=16] {'shot'}, dimensions={0} | all-to-all | bytes 2097152 | tf_op jit(solution)/shard_map/all_to_all | solution.py:348
  109.6 0.0 copy-done.1
  109.6 0.0 copy-done.2
  109.6 4.1 %update.1 = (f32[64,16,256]{2,1,0:T(8,128)}, f32[64,16,256]{2,1,0:T(8,128)}) custom-call(s32[16,128]{1,0:T(8,128)S(1)} %bitcast.7, f32[64,16,256]{2,1,0:T(8,128)S(1)} %all_to_all.22.returned, f32[64,16,256]{2,1,0:T(8,128)S(1)} %copy-done.1, f32[64,16,256]{2,1,0:T(8,128)S(1)} %copy-done.2), custom_call_target="tpu_custom_call" | custom-call | tf_op jit(solution)/shard_map/update/pallas_call | solution.py:353
  (10 shorter events, 0.0 us)
Async XLA Ops:
  15.2 1.2 %copy-start = (f32[64,16,256]{2,1,0:T(8,128)S(1)}, f32[64,16,256]{2,1,0:T(8,128)}, u32[]{:S(2)}) copy-start(f32[64,16,256]{2,1,0:T(8,128)} %velocity.3) | copy-start | bytes 3145732
  18.2 5.0 %copy-start.3 = (bf16[512,512]{1,0:T(8,128)(2,1)S(1)}, bf16[512,512]{1,0:T(8,128)(2,1)}, u32[]{:S(2)}) copy-start(bf16[512,512]{1,0:T(8,128)(2,1)} %constant.4.clone.same_ref) | copy-start | bytes 1572868
  18.2 5.0 %copy-start.10 = (bf16[256,256]{1,0:T(8,128)(2,1)S(1)}, bf16[256,256]{1,0:T(8,128)(2,1)}, u32[]{:S(2)}) copy-start(bf16[256,256]{1,0:T(8,128)(2,1)} %constant.5.clone.cross_ref) | copy-start | bytes 393220
  18.2 53.5 %all-to-all-start.1 = ((f32[64,16,256]{2,1,0:T(8,128)}), f32[64,16,256]{2,1,0:T(8,128)S(1)}, u32[]{:S(2)}, u32[]{:S(2)}) async-start(f32[64,16,256]{2,1,0:T(8,128)} %gather.1), calls=%async_computation.1 | async-start | bytes 2097152 | tf_op jit(solution)/shard_map/all_to_all | solution.py:321
  23.1 0.7 copy-start.15
  23.8 1.2 %copy-start.12 = (f32[1,2,32,32,128]{4,3,2,1,0:T(8,128)S(1)}, f32[1,2,32,32,128]{4,3,2,1,0:T(8,128)}, u32[]{:S(2)}) copy-start(f32[1,2,32,32,128]{4,3,2,1,0:T(8,128)} %param.15) | copy-start | bytes 3145732
  25.0 20.7 %copy-start.13 = (f32[1,2,8192]{2,1,0:T(2,128)S(1)}, f32[1,2,8192]{2,1,0:T(2,128)}, u32[]{:S(2)}) copy-start(f32[1,2,8192]{2,1,0:T(2,128)} %param.17) | copy-start | bytes 196612
  25.0 20.7 %copy-start.14 = (s32[1,8192]{1,0:T(1,128)S(1)}, s32[1,8192]{1,0:T(1,128)}, u32[]{:S(2)}) copy-start(s32[1,8192]{1,0:T(1,128)} %cells.1) | copy-start | bytes 98308
  69.3 0.8 copy-start.4
  70.1 0.8 copy-start.6
  70.9 0.8 copy-start.8
  71.7 0.7 copy-start.11
  72.3 1.0 copy-start.5
  73.4 1.0 copy-start.7
  74.4 1.0 copy-start.9
  78.4 31.2 %copy-start.1 = (f32[64,16,256]{2,1,0:T(8,128)S(1)}, f32[64,16,256]{2,1,0:T(8,128)}, u32[]{:S(2)}) copy-start(f32[64,16,256]{2,1,0:T(8,128)} %velocity.3) | copy-start | bytes 3145732
  78.4 31.2 %copy-start.2 = (f32[64,16,256]{2,1,0:T(8,128)S(1)}, f32[64,16,256]{2,1,0:T(8,128)}, u32[]{:S(2)}) copy-start(f32[64,16,256]{2,1,0:T(8,128)} %accumulated.1) | copy-start | bytes 3145732

commit v2 on v1

v2 whole, which is shorter than its diff:
```python
import functools

import jax
import jax.numpy as jnp
import numpy as np
from jax import lax
from jax.experimental import pallas as pl
from jax.experimental.pallas import tpu as pltpu
from jax.sharding import PartitionSpec as P

TS = 16
AX = 2
AY = 2
AZ = 8
BX = AX * TS
BY = AY * TS
APT = AX * AY * AZ
ROWS = BX * AZ
LANES = BY * TS
HALF = TS * TS
PAD = 4 * AZ
CHUNK = 2048
BLOCKS = 8
GROUPS = 4
HELD = 2**16

scaled_weights = (-14350.0, 8064.0, -1008.0, 128.0, -9.0)
weight_scale = 1.0 / 5040.0
step_rate = 0.02


def stencil_matrices():
    lane = np.arange(LANES)
    y, l = lane // TS, lane % TS
    same = np.zeros((LANES, LANES), np.float32)
    cross = np.zeros((LANES, LANES), np.float32)
    for offset in range(1, 5):
        w = scaled_weights[offset]
        dy = np.abs(y[:, None] - y[None, :])
        dl = np.abs(l[:, None] - l[None, :])
        same += w * ((dl == 0) & (dy == offset))
        same += w * ((dy == 0) & (dl == offset))
        cross += w * ((dy == 0) & (dl == TS - offset))
    return same, cross[:HALF, :HALF]


def split(value):
    high = value.astype(jnp.bfloat16)
    rest = value - high.astype(jnp.float32)
    middle = rest.astype(jnp.bfloat16)
    low = (rest - middle.astype(jnp.float32)).astype(jnp.bfloat16)
    return high, middle, low


def joined(ref, row, count):
    rows = slice(row, row + count)
    if len(ref.shape) == 2:
        return ref[rows, :]
    return jnp.concatenate([ref[part, rows, :] for part in range(ref.shape[0])], axis=1)


def stencil_products(field, parts, near, far, same_ref, cross_ref):
    for row in range(0, ROWS, 16):
        pieces = split(joined(field, PAD + row, 16))
        for p in range(3):
            parts[p, row : row + 16, :] = pieces[p]
    same = same_ref[...]
    cross = cross_ref[...]
    dot = functools.partial(jnp.dot, preferred_element_type=jnp.float32)
    near[...] = dot(parts[0], same) + dot(parts[1], same) + dot(parts[2], same)
    for side in range(0, LANES, HALF):
        cols = slice(side, side + HALF)
        far[:, cols] = (
            dot(parts[0, :, cols], cross) + dot(parts[1, :, cols], cross) + dot(parts[2, :, cols], cross)
        )


def laplacian_rows(field, near, far, row, upper, keep):
    at = PAD + row
    total = near[row : row + AZ, :] + 3.0 * scaled_weights[0] * joined(field, at, AZ)
    for offset in range(1, 5):
        pair = joined(field, at + offset * AZ, AZ) + joined(field, at - offset * AZ, AZ)
        total = total + scaled_weights[offset] * pair
    other = far[row : row + AZ, :]
    moved = jnp.where(upper, pltpu.roll(other, AZ - 1, 0), pltpu.roll(other, 1, 0))
    return weight_scale * (total + jnp.where(keep, moved, 0.0))


def far_masks():
    lane = lax.broadcasted_iota(jnp.int32, (AZ, LANES), 1) % TS
    row = lax.broadcasted_iota(jnp.int32, (AZ, LANES), 0)
    upper = lane >= TS // 2
    keep = row != jnp.where(upper, AZ - 1, 0)
    return upper, keep


def clear_pads(field):
    zero = jnp.zeros(field.shape[:-2] + (PAD, field.shape[-1]), jnp.float32)
    field[..., :PAD, :] = zero
    field[..., PAD + ROWS :, :] = zero


def slot_of(capacity, per_device, ids, k, counts):
    tile = ids[0, k]
    owner = tile // per_device
    rank = counts[owner]
    counts[owner] = rank + 1
    return owner * capacity + rank, tile - owner * per_device


def request_kernel(capacity, per_device, ids, table, counts):
    devices = table.shape[0]
    for owner in range(devices):
        counts[owner] = 0
    owner_of = lax.broadcasted_iota(jnp.int32, table.shape, 0)
    rank_of = lax.broadcasted_iota(jnp.int32, table.shape, 1)
    position = owner_of * capacity + jnp.where(rank_of < capacity, rank_of, -devices * capacity)
    found = jnp.full(table.shape, -1, jnp.int32)
    for k in range(APT):
        slot, tile = slot_of(capacity, per_device, ids, k, counts)
        found = jnp.where(position == slot, tile, found)
    table[...] = found


def gather_kernel(capacity, wanted_in, velocity, outgoing, wanted, owned, held, fetched, sent):
    devices = wanted_in.shape[0]
    listed = pltpu.make_async_copy(wanted_in, wanted, fetched.at[GROUPS])
    listed.start()
    tiles = velocity.shape[0] // GROUPS
    copies = [
        pltpu.make_async_copy(
            velocity.at[g * tiles : (g + 1) * tiles], owned.at[g * tiles : (g + 1) * tiles], fetched.at[g]
        )
        for g in range(GROUPS)
    ]
    for copy in copies:
        copy.start()
    listed.wait()
    for copy in copies:
        copy.wait()
    shots = devices // GROUPS
    copies = []
    for g in range(GROUPS):

        def step(shot, carry):
            for rank in range(capacity):
                held[shot * capacity + rank] = owned[jnp.maximum(wanted[shot, rank], 0)]
            return carry

        lax.fori_loop(g * shots, (g + 1) * shots, step, 0, unroll=True)
        part = slice(g * shots * capacity, (g + 1) * shots * capacity)
        copies.append(pltpu.make_async_copy(held.at[part], outgoing.at[part], sent.at[g]))
        copies[-1].start()
    for copy in copies:
        copy.wait()


def turn(start, step, x, y):
    group = lax.broadcasted_iota(jnp.int32, (8, 128), 1) // TS
    held = [start[step, pl.ds(x * BY + y + j, 8, BY), :] for j in range(8)]
    for bit in (1, 2, 4):
        low = (group & bit) == 0
        for j in range(8):
            if j & bit == 0:
                one, two = held[j], held[j + bit]
                held[j] = jnp.where(low, one, pltpu.roll(two, bit * TS, 1))
                held[j + bit] = jnp.where(low, pltpu.roll(one, 128 - bit * TS, 1), two)
    return held


def prepare(source, wavelet, start, same_ref, cross_ref, lap0, base1, base2, current, previous, parts, near, far):
    clear_pads(current)
    cell = source[0]
    sx, sy, sz = cell // (BY * AZ * TS), (cell // (AZ * TS)) % BY, cell % (AZ * TS)
    source_row = sx * AZ + sz // TS
    source_lane = sy * TS + sz % TS
    place = lax.broadcasted_iota(jnp.int32, (AZ, LANES), 0) * LANES + lax.broadcasted_iota(jnp.int32, (AZ, LANES), 1)

    for x in range(0, BX, 8):
        for y in range(0, BY, 8):
            old = turn(start, 0, x, y)
            new = turn(start, 1, x, y)
            for kz in range(AZ):
                previous[y // 8, pl.ds(x * AZ + kz, 8, AZ), :] = old[kz]
                current[y // 8, pl.ds(PAD + x * AZ + kz, 8, AZ), :] = new[kz]
    for x in range(BX):
        hit = place == (source_row - x * AZ) * LANES + source_lane
        rows = slice(x * AZ, x * AZ + AZ)
        now = joined(current, PAD + x * AZ, AZ)
        base1[rows, :] = 2.0 * now - joined(previous, x * AZ, AZ) + jnp.where(hit, wavelet[0, 0], 0.0)
        base2[rows, :] = jnp.where(hit, wavelet[0, 1], 0.0) - now
    stencil_products(current, parts, near, far, same_ref, cross_ref)
    upper, keep = far_masks()
    for x in range(BX):
        lap0[x * AZ : x * AZ + AZ, :] = laplacian_rows(current, near, far, x * AZ, upper, keep)


def local_kernel(
    capacity, per_device, cells, recorded, ids, source, wavelet, start, same_ref, cross_ref,
    fields_out, slots_out, same_out, cross_out,
    lap0, base1, base2, current, previous, parts, near, far, left, right, total, slots, counts, done,
):
    step = pl.program_id(0)
    last = pl.num_programs(0) - 1
    outputs = [
        (lap0, fields_out.at[:ROWS]),
        (base1, fields_out.at[ROWS : 2 * ROWS]),
        (base2, fields_out.at[2 * ROWS : 3 * ROWS]),
        (slots, slots_out.at[:1]),
        (same_ref, same_out.at[:LANES]),
        (cross_ref, cross_out.at[:HALF]),
    ]
    outputs = [pltpu.make_async_copy(a, b, done.at[n]) for n, (a, b) in enumerate(outputs)]

    @pl.when(step == 0)
    def _():
        total[...] = jnp.zeros_like(total)
        for owner in range(counts.shape[0]):
            counts[owner] = 0
        for k in range(APT):
            slots[0, k], _ = slot_of(capacity, per_device, ids, k, counts)
        prepare(source, wavelet, start, same_ref, cross_ref, lap0, base1, base2, current, previous, parts, near, far)
        for copy in outputs:
            copy.start()

    @pl.when(step < last)
    def _():
        here = pl.ds(pl.multiple_of(step * CHUNK, CHUNK), CHUNK)
        cell = cells[:, here]
        x, y, z = cell // (BY * AZ * TS), (cell // (AZ * TS)) % BY, cell % (AZ * TS)
        row = x * AZ + z // TS
        lane = y * TS + z % TS
        for at in range(0, LANES, 16):
            ids = lax.broadcasted_iota(jnp.int32, (16, CHUNK), 0) + at
            right[at : at + 16, :] = jnp.where(ids == lane, 1.0, 0.0).astype(jnp.bfloat16)
        pieces = []
        for n in range(2):
            pieces += split(jnp.broadcast_to(recorded[n : n + 1, here], (16, CHUNK)))
        for at in range(0, ROWS, 16):
            ids = lax.broadcasted_iota(jnp.int32, (16, CHUNK), 0) + at
            hot = jnp.where(ids == row, 1.0, 0.0).astype(jnp.bfloat16)
            left[at : at + 16, :] = hot
            for p in range(6):
                left[(p + 1) * ROWS + at : (p + 1) * ROWS + at + 16, :] = hot * pieces[p]
        total[...] += lax.dot_general(
            left[...], right[...], (((1,), (1,)), ((), ())), preferred_element_type=jnp.float32
        )

    @pl.when(step == last)
    def _():
        def part(n):
            return total[n * ROWS : (n + 1) * ROWS, :]

        total[ROWS : 2 * ROWS, :] = part(1) + part(2) + part(3)
        total[2 * ROWS : 3 * ROWS, :] = part(4) + part(5) + part(6)
        copy = pltpu.make_async_copy(total.at[: 3 * ROWS], fields_out.at[3 * ROWS : 6 * ROWS], done.at[6])
        copy.start()
        copy.wait()
        for copy in outputs:
            copy.wait()


def gradient_kernel(
    arrived, fields_in, slots_in, same_in, cross_in, outgoing,
    slots, same_ref, cross_ref, lap0, base1, base2, counts, sums0, sums1,
    courant, field1, field2, partial, parts, near, far, done,
):
    inputs = [(slots_in.at[:1], slots)]
    inputs += [
        (fields_in.at[n * ROWS : (n + 1) * ROWS], target)
        for n, target in enumerate((lap0, base1, base2, counts, sums0, sums1))
    ]
    inputs += [(same_in.at[:LANES], same_ref), (cross_in.at[:HALF], cross_ref)]
    copies = [pltpu.make_async_copy(a, b, done.at[n]) for n, (a, b) in enumerate(inputs)]
    for n in (0, 1, 2, 7, 8, 3, 4, 5, 6):
        copies[n].start()
    clear_pads(field1)
    clear_pads(field2)
    copies[0].wait()
    for k in range(APT):
        kx, ky, kz = k // (AY * AZ), (k // AZ) % AY, k % AZ
        tile = arrived[slots[0, k]]
        for part in range(2):
            courant[2 * ky + part, pl.ds(kx * TS * AZ + kz, TS, AZ), :] = tile[:, part * 128 : part * 128 + 128]
    copies[1].wait()
    copies[2].wait()
    for x in range(BX):
        rows = slice(x * AZ, x * AZ + AZ)
        speed = joined(courant, x * AZ, AZ)
        field1[PAD + x * AZ : PAD + x * AZ + AZ, :] = base1[rows, :] + speed * speed * lap0[rows, :]
    copies[7].wait()
    copies[8].wait()
    stencil_products(field1, parts, near, far, same_ref, cross_ref)
    upper, keep = far_masks()
    for copy in copies[3:7]:
        copy.wait()
    for x in range(BX):
        rows = slice(x * AZ, x * AZ + AZ)
        own = slice(PAD + x * AZ, PAD + x * AZ + AZ)
        speed = joined(courant, x * AZ, AZ)
        squared = speed * speed
        bent = laplacian_rows(field1, near, far, x * AZ, upper, keep)
        after = 2.0 * field1[own, :] + base2[rows, :] + squared * bent
        miss2 = counts[rows, :] * after - sums1[rows, :]
        field2[own, :] = squared * miss2
        base = counts[rows, :] * field1[own, :] - sums0[rows, :] + 2.0 * miss2
        partial[rows, :] = miss2 * bent + base * lap0[rows, :]
    stencil_products(field2, parts, near, far, same_ref, cross_ref)
    for x in range(BX):
        rows = slice(x * AZ, x * AZ + AZ)
        bent = laplacian_rows(field2, near, far, x * AZ, upper, keep)
        result = 2.0 * joined(courant, x * AZ, AZ) * (partial[rows, :] + bent * lap0[rows, :])
        for part in range(4):
            courant[part, rows, :] = result[:, part * 128 : part * 128 + 128]
    for k in range(APT):
        kx, ky, kz = k // (AY * AZ), (k // AZ) % AY, k % AZ
        for part in range(2):
            outgoing[slots[0, k], :, part * 128 : part * 128 + 128] = courant[
                2 * ky + part, pl.ds(kx * TS * AZ + kz, TS, AZ), :
            ]


def update_kernel(
    capacity, wanted, returned, velocity, accumulated, velocity_out, accumulated_out,
    pooled, new_velocity, new_accumulated, done,
):
    devices = wanted.shape[0]
    tiles = velocity.shape[0]
    zero = jnp.zeros(pooled.shape[1:], jnp.float32)
    for tile in range(tiles):
        pooled[tile] = zero

    def add(shot, carry):
        for rank in range(capacity):
            tile = wanted[shot, rank]
            tile = jnp.where(tile < 0, tiles, tile)
            pooled[tile] += returned[shot * capacity + rank]
        return carry

    lax.fori_loop(0, devices, add, 0, unroll=2)
    block = tiles // BLOCKS
    copies = []
    for n in range(BLOCKS):
        here = slice(n * block, (n + 1) * block)
        gradient = pooled[here]
        total = accumulated[here] + gradient * gradient
        new_accumulated[here] = total
        new_velocity[here] = velocity[here] - step_rate * gradient / jnp.sqrt(total)
        for which, (source, target) in enumerate(((new_velocity, velocity_out), (new_accumulated, accumulated_out))):
            copies.append(pltpu.make_async_copy(source.at[here], target.at[here], done.at[which, n]))
            copies[-1].start()
    for copy in copies:
        copy.wait()


VMEM = pl.BlockSpec(memory_space=pltpu.VMEM)
HBM = pl.BlockSpec(memory_space=pltpu.HBM)
SMEM = pl.BlockSpec(memory_space=pltpu.SMEM)
MIB = 2**20


def params(mib):
    return pltpu.CompilerParams(vmem_limit_bytes=mib * MIB)


def f32(*shape):
    return jax.ShapeDtypeStruct(shape, jnp.float32)


def body(velocity, accumulated, aperture_tiles, source_cell, wavelet, start_field, receiver_cells, observed):
    devices = lax.axis_size("shot")
    per_device = velocity.shape[0]
    capacity = max(2, 2 * APT // devices)
    same, cross = stencil_matrices()
    same = jnp.asarray(same, jnp.bfloat16)
    cross = jnp.asarray(cross, jnp.bfloat16)

    table = pl.pallas_call(
        functools.partial(request_kernel, capacity, per_device),
        out_shape=jax.ShapeDtypeStruct((devices, 128), jnp.int32),
        in_specs=[SMEM],
        out_specs=VMEM,
        scratch_shapes=[pltpu.SMEM((devices,), jnp.int32)],
        name="requests",
    )(aperture_tiles)
    wanted = lax.all_to_all(table, "shot", split_axis=0, concat_axis=0, tiled=True)

    fields = (ROWS, LANES)
    padded = pltpu.VMEM((ROWS + 2 * PAD, LANES), jnp.float32)
    whole = pltpu.VMEM(fields, jnp.float32)
    quarters = pltpu.VMEM((LANES // 128, ROWS, 128), jnp.float32)
    padded_quarters = pltpu.VMEM((LANES // 128, ROWS + 2 * PAD, 128), jnp.float32)
    pieces = pltpu.VMEM((3,) + fields, jnp.bfloat16)
    dma = pltpu.SemaphoreType.DMA
    slots_total = devices * capacity
    held = pltpu.VMEM((slots_total,) + velocity.shape[1:], jnp.float32)
    owned = pltpu.VMEM(velocity.shape, jnp.float32)
    outgoing = pl.pallas_call(
        functools.partial(gather_kernel, capacity),
        out_shape=f32(slots_total, *velocity.shape[1:]),
        in_specs=[HBM, HBM],
        out_specs=HBM,
        scratch_shapes=[pltpu.SMEM(wanted.shape, jnp.int32), owned, held, dma((GROUPS + 1,)), dma((GROUPS,))],
        compiler_params=params(62),
        name="gather",
    )(wanted, velocity)
    arrived = lax.all_to_all(outgoing, "shot", split_axis=0, concat_axis=0, tiled=True)

    receivers = receiver_cells.shape[1]
    list_memory = pltpu.SMEM((1, 128), jnp.int32)
    held_bytes = HELD * 128 * 4
    constants = [pltpu.VMEM(same.shape, same.dtype), pltpu.VMEM(cross.shape, cross.dtype)]
    fields_held, slots_held, same_held, cross_held = pl.pallas_call(
        functools.partial(local_kernel, capacity, per_device),
        out_shape=(
            f32(held_bytes // (4 * LANES), LANES),
            jax.ShapeDtypeStruct((held_bytes // (4 * 128), 128), jnp.int32),
            jax.ShapeDtypeStruct((held_bytes // (2 * LANES), LANES), jnp.bfloat16),
            jax.ShapeDtypeStruct((held_bytes // (2 * HALF), HALF), jnp.bfloat16),
        ),
        grid=(receivers // CHUNK + 1,),
        in_specs=[VMEM, VMEM, SMEM, SMEM, SMEM, VMEM, VMEM, VMEM],
        out_specs=(HBM,) * 4,
        scratch_shapes=[
            whole, whole, whole, padded_quarters, quarters, pieces, whole, whole,
            pltpu.VMEM((7 * ROWS, CHUNK), jnp.bfloat16),
            pltpu.VMEM((LANES, CHUNK), jnp.bfloat16),
            pltpu.VMEM((7 * ROWS, LANES), jnp.float32),
            list_memory,
            pltpu.SMEM((devices,), jnp.int32),
            dma((7,)),
        ],
        compiler_params=params(62),
        cost_estimate=pl.CostEstimate(flops=16 * 10**9, bytes_accessed=4 * MIB, transcendentals=0),
        name="local",
    )(
        receiver_cells, observed[0], aperture_tiles, source_cell, wavelet,
        start_field.reshape(2, BX * BY, AZ * TS), same, cross,
    )

    outgoing_gradient = pl.pallas_call(
        gradient_kernel,
        out_shape=f32(slots_total, *velocity.shape[1:]),
        in_specs=[VMEM, HBM, HBM, HBM, HBM],
        out_specs=VMEM,
        scratch_shapes=[
            list_memory, *constants, whole, whole, whole, whole, whole, whole,
            quarters, padded, padded, whole, pieces, whole, whole, dma((9,)),
        ],
        compiler_params=params(40),
        name="gradient",
    )(arrived, fields_held, slots_held, same_held, cross_held)
    returned = lax.all_to_all(outgoing_gradient, "shot", split_axis=0, concat_axis=0, tiled=True)

    tile = velocity.shape[1:]
    return pl.pallas_call(
        functools.partial(update_kernel, capacity),
        out_shape=(f32(*velocity.shape),) * 2,
        in_specs=[SMEM, VMEM, VMEM, VMEM],
        out_specs=(HBM,) * 2,
        scratch_shapes=[pltpu.VMEM((per_device + 1,) + tile, jnp.float32), owned, owned, dma((2, BLOCKS))],
        compiler_params=params(16),
        name="update",
    )(wanted, returned, velocity, accumulated)


def solution(mesh):
    split_shots = ("groups", "shot")
    return jax.shard_map(
        body,
        mesh=mesh,
        in_specs=(
            P(split_shots, None, None),
            P(split_shots, None, None),
            P(split_shots, None),
            P(split_shots),
            P(split_shots, None),
            P(split_shots, None, None, None, None),
            P(split_shots, None),
            P(split_shots, None, None),
        ),
        out_specs=(P(split_shots, None, None), P(split_shots, None, None)),
        check_vma=False,
    )
```

time: 114 us -> 83.3 us (0.73)
  Pallas kernels: 54.5 us -> 32.7 us
  local copies, waits for them, and re-layouts: 9.27 us -> 0.01 us
    pallas_call x3 -> x2, Pallas kernels: 47.1 us -> 26.4 us  [the longest x1 22.5 us: body(): pl.pallas_call(functools.partial(local_kernel, capacity, per_device), out...]
    unnamed x32 -> x6, local copies, waits for them, and re-layouts: 9.27 us -> 0.01 us
    pallas_call x1, Pallas kernels: 4.11 us -> 2.61 us  [body(): pl.pallas_call(functools.partial(update_kernel, capacity), out_shape=(f32...]
  transfers between devices with their start and end apart: 1 -> 1, of which waited for: 0 -> 1; matrix products, arithmetic and copies ran while one was open for 0% -> 0% of each run, Pallas kernels for 39% -> 27%
where the time goes in v2:
time: 83.3 us; the launch traced here: 83 us
  blocking collectives  44.8 us (54%)
  Pallas kernels  32.7 us (39%)
  starting transfers between devices  4.03 us (5%)
  between operations  1.31 us (2%)
    all_to_all x1, blocking collectives, body(): lax.all_to_all(outgoing_gradient, 'shot', split_axis=0, concat_axis=0, ti...  31.6 us
    pallas_call x1, Pallas kernels, body(): pl.pallas_call(functools.partial(local_kernel, capacity, per_device), out...  22.5 us
    all_to_all x1, blocking collectives, body(): lax.all_to_all(table, 'shot', split_axis=0, concat_axis=0, tiled=True)  13.2 us
    all_to_all x1, starting transfers between devices, body(): lax.all_to_all(outgoing, 'shot', split_axis=0, concat_axis=0, tiled=True)  4.03 us
    pallas_call x1, Pallas kernels, body(): pl.pallas_call(gradient_kernel, out_shape=f32(slots_total, *velocity.shap...  3.95 us
    pallas_call x1, Pallas kernels, body(): pl.pallas_call(functools.partial(update_kernel, capacity), out_shape=(f32...  2.61 us
    pallas_call x1, Pallas kernels, body(): pl.pallas_call(functools.partial(gather_kernel, capacity), out_shape=f32(...  2.24 us
  transfers between devices with their start and end apart: 1, of which 1 were waited for; matrix products, arithmetic and copies ran while one was open for 0% of the time, Pallas kernels for 27%

profile of v2, /device:TPU:1, one launch (start us, length us, event | category | flops | bytes accessed | tf_op | source)
XLA Modules:
  0.0 83.0 jit_solution(13423640061505853368)
XLA Ops:
  0.6 1.5 %requests.1 = s32[16,128]{1,0:T(8,128)} custom-call(s32[1,32]{1,0:T(1,128)} %ids.3), custom_call_target="tpu_custom_call" | custom-call | tf_op jit(solution)/shard_map/requests/pallas_call | solution.py:378
  2.1 13.2 %all_to_all.21 = s32[16,1,128]{2,1,0:T(1,128)} all-to-all(s32[16,1,128]{2,1,0:T(1,128)} %bitcast.8), channel_id=1, replica_groups=mesh['groups'=2,'shot'=16] {'shot'}, dimensions={0} | all-to-all | bytes 16384 | tf_op jit(solution)/shard_map/all_to_all | solution.py:386
  15.3 2.2 %gather.1 = f32[64,16,256]{2,1,0:T(8,128)} custom-call(s32[16,128]{1,0:T(8,128)} %bitcast.6, f32[64,16,256]{2,1,0:T(8,128)} %velocity.3), custom_call_target="tpu_custom_call" | custom-call | tf_op jit(solution)/shard_map/gather/pallas_call | solution.py:398
  17.5 4.0 %all-to-all-start.1 = ((f32[64,16,256]{2,1,0:T(8,128)}), f32[64,16,256]{2,1,0:T(8,128)S(1)}, u32[]{:S(2)}, u32[]{:S(2)}) async-start(f32[64,16,256]{2,1,0:T(8,128)} %gather.1), calls=%async_computation.1 | async-start | bytes 2097152 | tf_op jit(solution)/shard_map/all_to_all | solution.py:407
  22.2 22.5 %local.1 = (f32[16384,512]{1,0:T(8,128)}, s32[65536,128]{1,0:T(8,128)}, bf16[32768,512]{1,0:T(8,128)(2,1)}, bf16[65536,256]{1,0:T(8,128)(2,1)}) custom-call(s32[1,8192]{1,0:T(1,128)} %cells.1, f32[2,8192]{1,0:T(2,128)} %bitcast.10, s32[1,32]{1,0:T(1,128)} %ids.3, s32[1]{0:T(128)S(6)} %copy.13.source, f32[1,2]{1,0:T(1,128)} %wavelet.1, ...), custom_call_target="tpu_custom_call" | custom-call | flops 16000000000 | bytes 4194304 | tf_op jit(solution)/shard_map/local/pallas_call | solution.py:413
  44.7 0.1 all-to-all-done.1.arrived
  44.7 0.0 copy-start
  44.7 0.0 copy-start.1
  44.7 0.0 copy-start.2
  44.7 3.9 %gradient.1 = f32[64,16,256]{2,1,0:T(8,128)S(1)} custom-call(f32[64,16,256]{2,1,0:T(8,128)S(1)} %all-to-all-done.1.arrived, f32[16384,512]{1,0:T(8,128)} %get-tuple-element.6.fields_in, s32[65536,128]{1,0:T(8,128)} %get-tuple-element.7.slots_in, bf16[32768,512]{1,0:T(8,128)(2,1)} %get-tuple-element.8.same_in, bf16[65536,256]{1,0:T(8,128)(2,1)} %get-tuple-element.9.cross_in), custom_call_target="tpu_custom_call" | custom-call | tf_op jit(solution)/shard_map/gradient/pallas_call | solution.py:441
  48.7 31.6 %all_to_all.22.returned = f32[64,16,256]{2,1,0:T(8,128)S(1)} all-to-all(f32[64,16,256]{2,1,0:T(8,128)S(1)} %gradient.1), channel_id=1, replica_groups=mesh['groups'=2,'shot'=16] {'shot'}, dimensions={0} | all-to-all | bytes 2097152 | tf_op jit(solution)/shard_map/all_to_all | solution.py:453
  80.3 0.0 copy-done
  80.3 0.0 copy-done.1
  80.3 0.0 copy-done.2
  80.4 2.6 %update.1 = (f32[64,16,256]{2,1,0:T(8,128)}, f32[64,16,256]{2,1,0:T(8,128)}) custom-call(s32[16,128]{1,0:T(8,128)S(1)} %bitcast.7, f32[64,16,256]{2,1,0:T(8,128)S(1)} %all_to_all.22.returned, f32[64,16,256]{2,1,0:T(8,128)S(1)} %copy-done, f32[64,16,256]{2,1,0:T(8,128)S(1)} %copy-done.1), custom_call_target="tpu_custom_call" | custom-call | tf_op jit(solution)/shard_map/update/pallas_call | solution.py:456
Async XLA Ops:
  17.5 27.2 %all-to-all-start.1 = ((f32[64,16,256]{2,1,0:T(8,128)}), f32[64,16,256]{2,1,0:T(8,128)S(1)}, u32[]{:S(2)}, u32[]{:S(2)}) async-start(f32[64,16,256]{2,1,0:T(8,128)} %gather.1), calls=%async_computation.1 | async-start | bytes 2097152 | tf_op jit(solution)/shard_map/all_to_all | solution.py:407
  44.7 35.6 %copy-start = (f32[64,16,256]{2,1,0:T(8,128)S(1)}, f32[64,16,256]{2,1,0:T(8,128)}, u32[]{:S(2)}) copy-start(f32[64,16,256]{2,1,0:T(8,128)} %velocity.3) | copy-start | bytes 3145732
  44.7 35.6 %copy-start.1 = (f32[64,16,256]{2,1,0:T(8,128)S(1)}, f32[64,16,256]{2,1,0:T(8,128)}, u32[]{:S(2)}) copy-start(f32[64,16,256]{2,1,0:T(8,128)} %accumulated.1) | copy-start | bytes 3145732
  44.7 35.6 %copy-start.2 = (s32[16,1,128]{2,1,0:T(1,128)S(1)}, s32[16,1,128]{2,1,0:T(1,128)}, u32[]{:S(2)}) copy-start(s32[16,1,128]{2,1,0:T(1,128)} %all_to_all.21) | copy-start | bytes 24580

commit v3 on v2

v3 whole, which is shorter than its diff:
```python
import functools

import jax
import jax.numpy as jnp
import numpy as np
from jax import lax
from jax.experimental import pallas as pl
from jax.experimental.pallas import tpu as pltpu
from jax.sharding import PartitionSpec as P

TS = 16
AX = 2
AY = 2
AZ = 8
BX = AX * TS
BY = AY * TS
APT = AX * AY * AZ
ROWS = BX * AZ
LANES = BY * TS
HALF = TS * TS
BLOCKS = 8
GROUPS = 4
HELD = 2**16

scaled_weights = (-14350.0, 8064.0, -1008.0, 128.0, -9.0)
weight_scale = 1.0 / 5040.0
step_rate = 0.02


def stencil_matrices():
    lane = np.arange(LANES)
    y, l = lane // TS, lane % TS
    same = np.zeros((LANES, LANES), np.float32)
    cross = np.zeros((LANES, LANES), np.float32)
    for offset in range(1, 5):
        w = scaled_weights[offset]
        dy = np.abs(y[:, None] - y[None, :])
        dl = np.abs(l[:, None] - l[None, :])
        same += w * ((dl == 0) & (dy == offset))
        same += w * ((dy == 0) & (dl == offset))
        cross += w * ((dy == 0) & (dl == TS - offset))
    row = np.arange(ROWS)
    x, kz = row // (AZ * TS) * TS + row % TS, row // TS % AZ
    down = np.zeros((ROWS, ROWS), np.float32)
    for offset in range(1, 5):
        distance = np.abs(x[:, None] - x[None, :])
        down += scaled_weights[offset] * ((kz[:, None] == kz[None, :]) & (distance == offset))
    return same, np.concatenate([cross[:HALF, :HALF], down], axis=0)


def split(value):
    high = value.astype(jnp.bfloat16)
    rest = value - high.astype(jnp.float32)
    middle = rest.astype(jnp.bfloat16)
    low = (rest - middle.astype(jnp.float32)).astype(jnp.bfloat16)
    return high, middle, low


def stencil_products(field, parts, near, far, same_ref, cross_ref):
    for row in range(0, ROWS, 16):
        pieces = split(field[row : row + 16, :])
        for p in range(3):
            parts[p, row : row + 16, :] = pieces[p]
    same = same_ref[...]
    cross = cross_ref[:HALF, :]
    down = cross_ref[HALF:, :]
    dot = functools.partial(jnp.dot, preferred_element_type=jnp.float32)
    near[...] = dot(parts[0], same) + dot(parts[1], same) + dot(parts[2], same)
    near[...] += dot(down, parts[0]) + dot(down, parts[1]) + dot(down, parts[2])
    for side in range(0, LANES, HALF):
        cols = slice(side, side + HALF)
        far[:, cols] = (
            dot(parts[0, :, cols], cross) + dot(parts[1, :, cols], cross) + dot(parts[2, :, cols], cross)
        )


def laplacian_rows(field, near, far, row, upper):
    total = near[row : row + 8, :] + 3.0 * scaled_weights[0] * field[row : row + 8, :]
    kz = row // TS % AZ
    zero = jnp.zeros((8, LANES), jnp.float32)
    after = far[row + TS : row + TS + 8, :] if kz < AZ - 1 else zero
    before = far[row - TS : row - TS + 8, :] if kz > 0 else zero
    return weight_scale * (total + jnp.where(upper, after, before))


def upper_half():
    return lax.broadcasted_iota(jnp.int32, (8, LANES), 1) % TS >= TS // 2


def tile_row(x, z):
    return (x // TS * AZ + z // TS) * TS + x % TS


def slot_of(capacity, per_device, ids, k, counts):
    tile = ids[0, k]
    owner = tile // per_device
    rank = counts[owner]
    counts[owner] = rank + 1
    return owner * capacity + rank, tile - owner * per_device


def request_kernel(capacity, per_device, ids, table, counts):
    devices = table.shape[0]
    for owner in range(devices):
        counts[owner] = 0
    owner_of = lax.broadcasted_iota(jnp.int32, table.shape, 0)
    rank_of = lax.broadcasted_iota(jnp.int32, table.shape, 1)
    position = owner_of * capacity + jnp.where(rank_of < capacity, rank_of, -devices * capacity)
    found = jnp.full(table.shape, -1, jnp.int32)
    for k in range(APT):
        slot, tile = slot_of(capacity, per_device, ids, k, counts)
        found = jnp.where(position == slot, tile, found)
    table[...] = found


def gather_kernel(capacity, wanted_in, velocity, outgoing, wanted, owned, held, fetched, sent):
    devices = wanted_in.shape[0]
    listed = pltpu.make_async_copy(wanted_in, wanted, fetched.at[GROUPS])
    listed.start()
    tiles = velocity.shape[0] // GROUPS
    copies = [
        pltpu.make_async_copy(
            velocity.at[g * tiles : (g + 1) * tiles], owned.at[g * tiles : (g + 1) * tiles], fetched.at[g]
        )
        for g in range(GROUPS)
    ]
    for copy in copies:
        copy.start()
    listed.wait()
    for copy in copies:
        copy.wait()
    shots = devices // GROUPS
    copies = []
    for g in range(GROUPS):

        def step(shot, carry):
            for rank in range(capacity):
                held[shot * capacity + rank] = owned[jnp.maximum(wanted[shot, rank], 0)]
            return carry

        lax.fori_loop(g * shots, (g + 1) * shots, step, 0, unroll=True)
        part = slice(g * shots * capacity, (g + 1) * shots * capacity)
        copies.append(pltpu.make_async_copy(held.at[part], outgoing.at[part], sent.at[g]))
        copies[-1].start()
    for copy in copies:
        copy.wait()


def turn(start, step, x, y):
    group = lax.broadcasted_iota(jnp.int32, (8, 128), 1) // TS
    held = [start[step, pl.ds(x * BY + y + j, 8, BY), :] for j in range(8)]
    for bit in (1, 2, 4):
        low = (group & bit) == 0
        for j in range(8):
            if j & bit == 0:
                one, two = held[j], held[j + bit]
                held[j] = jnp.where(low, one, pltpu.roll(two, bit * TS, 1))
                held[j + bit] = jnp.where(low, pltpu.roll(one, 128 - bit * TS, 1), two)
    return held


def local_kernel(
    capacity, per_device, cells, recorded, ids, source, wavelet, start_in, same_ref, cross_ref,
    fields_out, slots_out, same_out, cross_out,
    start, lap0, base1, base2, current, parts, near, far, left, right, total, slots, counts, done,
):
    step = pl.program_id(0)
    last = pl.num_programs(0) - 1
    chunk = left.shape[1]

    def copy_of(n, held, target):
        return pltpu.make_async_copy(held, target, done.at[n])

    lists = [
        copy_of(0, slots, slots_out.at[:1]),
        copy_of(1, same_ref, same_out.at[:LANES]),
        copy_of(2, cross_ref, cross_out.at[: HALF + ROWS]),
    ]
    bases = [copy_of(3, base1, fields_out.at[ROWS : 2 * ROWS])]
    results = [
        copy_of(4, total.at[: 3 * ROWS], fields_out.at[2 * ROWS : 5 * ROWS]),
        copy_of(5, lap0, fields_out.at[:ROWS]),
    ]

    @pl.when(step == 0)
    def _():
        copies = [copy_of(6 + n, start_in.at[n], start.at[n, : BX * BY]) for n in range(2)]
        for copy in copies:
            copy.start()
        total[...] = jnp.zeros_like(total)
        for owner in range(counts.shape[0]):
            counts[owner] = 0
        for k in range(APT):
            slots[0, k], _ = slot_of(capacity, per_device, ids, k, counts)
        for copy in lists:
            copy.start()
        for copy in copies:
            copy.wait()

    @pl.when(step < last)
    def _():
        here = pl.ds(pl.multiple_of(step * chunk, chunk), chunk)
        cell = cells[:, here]
        x, y, z = cell // (BY * AZ * TS), (cell // (AZ * TS)) % BY, cell % (AZ * TS)
        row = tile_row(x, z)
        lane = y * TS + z % TS
        for at in range(0, LANES, 16):
            numbers = lax.broadcasted_iota(jnp.int32, (16, chunk), 0) + at
            right[at : at + 16, :] = jnp.where(numbers == lane, 1.0, 0.0).astype(jnp.bfloat16)
        pieces = []
        for n in range(2):
            pieces += split(jnp.broadcast_to(recorded[n : n + 1, here], (16, chunk)))
        for at in range(0, ROWS, 16):
            numbers = lax.broadcasted_iota(jnp.int32, (16, chunk), 0) + at
            hot = jnp.where(numbers == row, 1.0, 0.0).astype(jnp.bfloat16)
            left[at : at + 16, :] = hot
            for p in range(6):
                left[(p + 1) * ROWS + at : (p + 1) * ROWS + at + 16, :] = hot * pieces[p]
        total[...] += lax.dot_general(
            left[...], right[...], (((1,), (1,)), ((), ())), preferred_element_type=jnp.float32
        )

        cell = source[0]
        sx, sy, sz = cell // (BY * AZ * TS), (cell // (AZ * TS)) % BY, cell % (AZ * TS)
        source_row = tile_row(sx, sz)
        source_lane = sy * TS + sz % TS
        place = lax.broadcasted_iota(jnp.int32, (8, LANES), 0) * LANES + lax.broadcasted_iota(
            jnp.int32, (8, LANES), 1
        )
        first = step * 8
        old = [turn(start, 0, first, y) for y in range(0, BY, 8)]
        new = [turn(start, 1, first, y) for y in range(0, BY, 8)]
        for kz in range(AZ):
            at = pl.multiple_of((first // TS * AZ + kz) * TS + first % TS, 8)
            hit = place == (source_row - at) * LANES + source_lane
            rows = pl.ds(at, 8)
            now = jnp.concatenate([part[kz] for part in new], axis=1)
            before = jnp.concatenate([part[kz] for part in old], axis=1)
            current[rows, :] = now
            base1[rows, :] = 2.0 * now - before + jnp.where(hit, wavelet[0, 0], 0.0)
            base2[rows, :] = jnp.where(hit, wavelet[0, 1], 0.0) - now

    @pl.when(step == last)
    def _():
        for copy in bases:
            copy.start()

        def part(n):
            return total[n * ROWS : (n + 1) * ROWS, :]

        total[ROWS : 2 * ROWS, :] = part(1) + part(2) + part(3)
        total[2 * ROWS : 3 * ROWS, :] = part(0) * base2[...] - (part(4) + part(5) + part(6))
        results[0].start()
        stencil_products(current, parts, near, far, same_ref, cross_ref)
        upper = upper_half()
        for row in range(0, ROWS, 8):
            lap0[row : row + 8, :] = laplacian_rows(current, near, far, row, upper)
        results[1].start()
        for copy in lists + bases + results:
            copy.wait()


def gradient_kernel(
    arrived, fields_in, slots_in, same_in, cross_in, outgoing,
    slots, same_ref, cross_ref, lap0, base1, counts, sums0, known1,
    courant, field1, field2, partial, parts, near, far, done,
):
    inputs = [(slots_in.at[:1], slots)]
    inputs += [
        (fields_in.at[n * ROWS : (n + 1) * ROWS], target)
        for n, target in enumerate((lap0, base1, counts, sums0, known1))
    ]
    inputs += [(same_in.at[:LANES], same_ref), (cross_in.at[: HALF + ROWS], cross_ref)]
    copies = [pltpu.make_async_copy(a, b, done.at[n]) for n, (a, b) in enumerate(inputs)]
    for n in (0, 1, 2, 6, 7, 3, 5, 4):
        copies[n].start()
    copies[0].wait()
    copies[1].wait()
    copies[2].wait()
    for k in range(APT):
        kx, ky, kz = k // (AY * AZ), (k // AZ) % AY, k % AZ
        rows = slice((kx * AZ + kz) * TS, (kx * AZ + kz + 1) * TS)
        cols = slice(ky * HALF, (ky + 1) * HALF)
        speed = arrived[slots[0, k]]
        courant[rows, cols] = speed
        field1[rows, cols] = base1[rows, cols] + speed * speed * lap0[rows, cols]
    copies[6].wait()
    copies[7].wait()
    stencil_products(field1, parts, near, far, same_ref, cross_ref)
    upper = upper_half()
    for copy in copies[3:6]:
        copy.wait()
    for row in range(0, ROWS, 8):
        rows = slice(row, row + 8)
        speed = courant[rows, :]
        squared = speed * speed
        bent = laplacian_rows(field1, near, far, row, upper)
        miss2 = counts[rows, :] * (2.0 * field1[rows, :] + squared * bent) + known1[rows, :]
        field2[rows, :] = squared * miss2
        base = counts[rows, :] * field1[rows, :] - sums0[rows, :] + 2.0 * miss2
        partial[rows, :] = miss2 * bent + base * lap0[rows, :]
    stencil_products(field2, parts, near, far, same_ref, cross_ref)
    for kx in range(AX):
        for kz in range(AZ):
            for half in range(0, TS, 8):
                row = (kx * AZ + kz) * TS + half
                rows = slice(row, row + 8)
                bent = laplacian_rows(field2, near, far, row, upper)
                result = 2.0 * courant[rows, :] * (partial[rows, :] + bent * lap0[rows, :])
                for ky in range(AY):
                    slot = slots[0, (kx * AY + ky) * AZ + kz]
                    outgoing[slot, half : half + 8, :] = result[:, ky * HALF : (ky + 1) * HALF]


def update_kernel(
    capacity, wanted_in, returned, velocity, accumulated, velocity_out, accumulated_out,
    wanted, pooled, new_velocity, new_accumulated, listed, done,
):
    devices = wanted.shape[0]
    tiles = velocity.shape[0]
    copy = pltpu.make_async_copy(wanted_in, wanted, listed)
    copy.start()
    zero = jnp.zeros(pooled.shape[1:], jnp.float32)
    for tile in range(tiles):
        pooled[tile] = zero
    copy.wait()

    def add(shot, carry):
        for rank in range(capacity):
            tile = wanted[shot, rank]
            tile = jnp.where(tile < 0, tiles, tile)
            pooled[tile] += returned[shot * capacity + rank]
        return carry

    lax.fori_loop(0, devices, add, 0, unroll=8)
    block = tiles // BLOCKS
    copies = []
    for n in range(BLOCKS):
        here = slice(n * block, (n + 1) * block)
        gradient = pooled[here]
        total = accumulated[here] + gradient * gradient
        new_accumulated[here] = total
        new_velocity[here] = velocity[here] - step_rate * gradient * lax.rsqrt(total)
        for which, (source, target) in enumerate(((new_velocity, velocity_out), (new_accumulated, accumulated_out))):
            copies.append(pltpu.make_async_copy(source.at[here], target.at[here], done.at[which, n]))
            copies[-1].start()
    for copy in copies:
        copy.wait()


VMEM = pl.BlockSpec(memory_space=pltpu.VMEM)
HBM = pl.BlockSpec(memory_space=pltpu.HBM)
SMEM = pl.BlockSpec(memory_space=pltpu.SMEM)
MIB = 2**20


def params(mib):
    return pltpu.CompilerParams(vmem_limit_bytes=mib * MIB)


def f32(*shape):
    return jax.ShapeDtypeStruct(shape, jnp.float32)


def body(velocity, accumulated, aperture_tiles, source_cell, wavelet, start_field, receiver_cells, observed):
    devices = lax.axis_size("shot")
    per_device = velocity.shape[0]
    capacity = max(2, 2 * APT // devices)
    same, cross = stencil_matrices()
    same = jnp.asarray(same, jnp.bfloat16)
    cross = jnp.asarray(cross, jnp.bfloat16)

    table = pl.pallas_call(
        functools.partial(request_kernel, capacity, per_device),
        out_shape=jax.ShapeDtypeStruct((devices, 128), jnp.int32),
        in_specs=[SMEM],
        out_specs=VMEM,
        scratch_shapes=[pltpu.SMEM((devices,), jnp.int32)],
        name="requests",
    )(aperture_tiles)
    wanted = lax.all_to_all(table, "shot", split_axis=0, concat_axis=0, tiled=True)

    fields = (ROWS, LANES)
    whole = pltpu.VMEM(fields, jnp.float32)
    pieces = pltpu.VMEM((3,) + fields, jnp.bfloat16)
    dma = pltpu.SemaphoreType.DMA
    slots_total = devices * capacity
    held = pltpu.VMEM((slots_total,) + velocity.shape[1:], jnp.float32)
    owned = pltpu.VMEM(velocity.shape, jnp.float32)
    outgoing = pl.pallas_call(
        functools.partial(gather_kernel, capacity),
        out_shape=f32(slots_total, *velocity.shape[1:]),
        in_specs=[HBM, HBM],
        out_specs=HBM,
        scratch_shapes=[pltpu.SMEM(wanted.shape, jnp.int32), owned, held, dma((GROUPS + 1,)), dma((GROUPS,))],
        compiler_params=params(62),
        name="gather",
    )(wanted, velocity)
    arrived = lax.all_to_all(outgoing, "shot", split_axis=0, concat_axis=0, tiled=True)

    chunk = receiver_cells.shape[1] // (BX // 8)
    list_memory = pltpu.SMEM((1, 128), jnp.int32)
    held_bytes = HELD * 128 * 4
    constants = [pltpu.VMEM(same.shape, same.dtype), pltpu.VMEM(cross.shape, cross.dtype)]
    fields_held, slots_held, same_held, cross_held = pl.pallas_call(
        functools.partial(local_kernel, capacity, per_device),
        out_shape=(
            f32(held_bytes // (4 * LANES), LANES),
            jax.ShapeDtypeStruct((held_bytes // (4 * 128), 128), jnp.int32),
            jax.ShapeDtypeStruct((held_bytes // (2 * LANES), LANES), jnp.bfloat16),
            jax.ShapeDtypeStruct((held_bytes // (2 * HALF), HALF), jnp.bfloat16),
        ),
        grid=(BX // 8 + 1,),
        in_specs=[VMEM, VMEM, SMEM, SMEM, SMEM, HBM, VMEM, VMEM],
        out_specs=(HBM,) * 4,
        scratch_shapes=[
            pltpu.VMEM((2, BX * BY + 8 * BY, AZ * TS), jnp.float32),
            whole, whole, whole, whole, pieces, whole, whole,
            pltpu.VMEM((7 * ROWS, chunk), jnp.bfloat16),
            pltpu.VMEM((LANES, chunk), jnp.bfloat16),
            pltpu.VMEM((7 * ROWS, LANES), jnp.float32),
            list_memory,
            pltpu.SMEM((devices,), jnp.int32),
            dma((8,)),
        ],
        compiler_params=params(62),
        cost_estimate=pl.CostEstimate(flops=16 * 10**9, bytes_accessed=4 * MIB, transcendentals=0),
        name="local",
    )(
        receiver_cells, observed[0], aperture_tiles, source_cell, wavelet,
        start_field.reshape(2, BX * BY, AZ * TS), same, cross,
    )

    outgoing_gradient = pl.pallas_call(
        gradient_kernel,
        out_shape=f32(slots_total, *velocity.shape[1:]),
        in_specs=[VMEM, HBM, HBM, HBM, HBM],
        out_specs=VMEM,
        scratch_shapes=[
            list_memory, *constants, whole, whole, whole, whole, whole,
            whole, whole, whole, whole, pieces, whole, whole, dma((8,)),
        ],
        compiler_params=params(40),
        name="gradient",
    )(arrived, fields_held, slots_held, same_held, cross_held)
    returned = lax.all_to_all(outgoing_gradient, "shot", split_axis=0, concat_axis=0, tiled=True)

    tile = velocity.shape[1:]
    return pl.pallas_call(
        functools.partial(update_kernel, capacity),
        out_shape=(f32(*velocity.shape),) * 2,
        in_specs=[HBM, VMEM, VMEM, VMEM],
        out_specs=(HBM,) * 2,
        scratch_shapes=[
            pltpu.SMEM(wanted.shape, jnp.int32),
            pltpu.VMEM((per_device + 1,) + tile, jnp.float32),
            owned, owned, dma, dma((2, BLOCKS)),
        ],
        compiler_params=params(16),
        name="update",
    )(wanted, returned, velocity, accumulated)


def solution(mesh):
    split_shots = ("groups", "shot")
    return jax.shard_map(
        body,
        mesh=mesh,
        in_specs=(
            P(split_shots, None, None),
            P(split_shots, None, None),
            P(split_shots, None),
            P(split_shots),
            P(split_shots, None),
            P(split_shots, None, None, None, None),
            P(split_shots, None),
            P(split_shots, None, None),
        ),
        out_specs=(P(split_shots, None, None), P(split_shots, None, None)),
        check_vma=False,
    )
```

time: 83.3 us -> 83.2 us (level)
  transfers between devices with their start and end apart: 1 -> 1, of which waited for: 1 -> 1; matrix products, arithmetic and copies ran while one was open for 0% -> 0% of each run, Pallas kernels for 27% -> 26%
where the time goes in v3:
time: 83.2 us; the launch traced here: 82.8 us
  blocking collectives  44.8 us (54%)
  Pallas kernels  32.1 us (39%)
  starting transfers between devices  4.03 us (5%)
  between operations  1.31 us (2%)
    all_to_all x1, blocking collectives, body(): lax.all_to_all(outgoing_gradient, 'shot', split_axis=0, concat_axis=0, ti...  31.6 us
    pallas_call x1, Pallas kernels, body(): pl.pallas_call(functools.partial(local_kernel, capacity, per_device), out...  21.9 us
    all_to_all x1, blocking collectives, body(): lax.all_to_all(table, 'shot', split_axis=0, concat_axis=0, tiled=True)  13.2 us
    all_to_all x1, starting transfers between devices, body(): lax.all_to_all(outgoing, 'shot', split_axis=0, concat_axis=0, tiled=True)  4.03 us
    pallas_call x1, Pallas kernels, body(): pl.pallas_call(gradient_kernel, out_shape=f32(slots_total, *velocity.shap...  3.92 us
    pallas_call x1, Pallas kernels, body(): pl.pallas_call(functools.partial(update_kernel, capacity), out_shape=(f32...  2.53 us
    pallas_call x1, Pallas kernels, body(): pl.pallas_call(functools.partial(gather_kernel, capacity), out_shape=f32(...  2.24 us
  transfers between devices with their start and end apart: 1, of which 1 were waited for; matrix products, arithmetic and copies ran while one was open for 0% of the time, Pallas kernels for 26%

profile of v3, /device:TPU:1, one launch (start us, length us, event | category | flops | bytes accessed | tf_op | source)
XLA Modules:
  0.0 82.8 jit_solution(12351649738898615258)
XLA Ops:
  0.6 1.5 %requests.1 = s32[16,128]{1,0:T(8,128)} custom-call(s32[1,32]{1,0:T(1,128)} %ids.3), custom_call_target="tpu_custom_call" | custom-call | tf_op jit(solution)/shard_map/requests/pallas_call | solution.py:373
  2.1 13.2 %all_to_all.21 = s32[16,1,128]{2,1,0:T(1,128)} all-to-all(s32[16,1,128]{2,1,0:T(1,128)} %bitcast.8), channel_id=1, replica_groups=mesh['groups'=2,'shot'=16] {'shot'}, dimensions={0} | all-to-all | bytes 16384 | tf_op jit(solution)/shard_map/all_to_all | solution.py:381
  15.3 2.2 %gather.1 = f32[64,16,256]{2,1,0:T(8,128)} custom-call(s32[16,128]{1,0:T(8,128)} %bitcast.6, f32[64,16,256]{2,1,0:T(8,128)} %velocity.3), custom_call_target="tpu_custom_call" | custom-call | tf_op jit(solution)/shard_map/gather/pallas_call | solution.py:390
  17.5 4.0 %all-to-all-start.1 = ((f32[64,16,256]{2,1,0:T(8,128)}), f32[64,16,256]{2,1,0:T(8,128)S(1)}, u32[]{:S(2)}, u32[]{:S(2)}) async-start(f32[64,16,256]{2,1,0:T(8,128)} %gather.1), calls=%async_computation.1 | async-start | bytes 2097152 | tf_op jit(solution)/shard_map/all_to_all | solution.py:399
  22.2 21.9 %local.1 = (f32[16384,512]{1,0:T(8,128)}, s32[65536,128]{1,0:T(8,128)}, bf16[32768,512]{1,0:T(8,128)(2,1)}, bf16[65536,256]{1,0:T(8,128)(2,1)}) custom-call(s32[1,8192]{1,0:T(1,128)} %cells.1, f32[2,8192]{1,0:T(2,128)} %bitcast.10, s32[1,32]{1,0:T(1,128)} %ids.3, s32[1]{0:T(128)S(6)} %copy.13.source, f32[1,2]{1,0:T(1,128)} %wavelet.1, ...), custom_call_target="tpu_custom_call" | custom-call | flops 16000000000 | bytes 4194304 | tf_op jit(solution)/shard_map/local/pallas_call | solution.py:405
  44.1 0.6 all-to-all-done.1.arrived
  44.7 0.0 copy-start
  44.7 0.0 copy-start.1
  44.7 0.0 copy-start.2
  44.7 3.9 %gradient.1 = f32[64,16,256]{2,1,0:T(8,128)S(1)} custom-call(f32[64,16,256]{2,1,0:T(8,128)S(1)} %all-to-all-done.1.arrived, f32[16384,512]{1,0:T(8,128)} %get-tuple-element.6.fields_in, s32[65536,128]{1,0:T(8,128)} %get-tuple-element.7.slots_in, bf16[32768,512]{1,0:T(8,128)(2,1)} %get-tuple-element.8.same_in, bf16[65536,256]{1,0:T(8,128)(2,1)} %get-tuple-element.9.cross_in), custom_call_target="tpu_custom_call" | custom-call | tf_op jit(solution)/shard_map/gradient/pallas_call | solution.py:434
  48.7 31.6 %all_to_all.22.returned = f32[64,16,256]{2,1,0:T(8,128)S(1)} all-to-all(f32[64,16,256]{2,1,0:T(8,128)S(1)} %gradient.1), channel_id=1, replica_groups=mesh['groups'=2,'shot'=16] {'shot'}, dimensions={0} | all-to-all | bytes 2097152 | tf_op jit(solution)/shard_map/all_to_all | solution.py:446
  80.3 0.0 copy-done
  80.3 0.0 copy-done.1
  80.3 0.0 copy-done.2
  80.3 2.5 %update.1 = (f32[64,16,256]{2,1,0:T(8,128)}, f32[64,16,256]{2,1,0:T(8,128)}) custom-call(s32[16,128]{1,0:T(8,128)S(1)} %bitcast.7, f32[64,16,256]{2,1,0:T(8,128)S(1)} %all_to_all.22.returned, f32[64,16,256]{2,1,0:T(8,128)S(1)} %copy-done, f32[64,16,256]{2,1,0:T(8,128)S(1)} %copy-done.1), custom_call_target="tpu_custom_call" | custom-call | tf_op jit(solution)/shard_map/update/pallas_call | solution.py:449
Async XLA Ops:
  17.5 27.2 %all-to-all-start.1 = ((f32[64,16,256]{2,1,0:T(8,128)}), f32[64,16,256]{2,1,0:T(8,128)S(1)}, u32[]{:S(2)}, u32[]{:S(2)}) async-start(f32[64,16,256]{2,1,0:T(8,128)} %gather.1), calls=%async_computation.1 | async-start | bytes 2097152 | tf_op jit(solution)/shard_map/all_to_all | solution.py:399
  44.7 35.6 %copy-start = (f32[64,16,256]{2,1,0:T(8,128)S(1)}, f32[64,16,256]{2,1,0:T(8,128)}, u32[]{:S(2)}) copy-start(f32[64,16,256]{2,1,0:T(8,128)} %velocity.3) | copy-start | bytes 3145732
  44.7 35.6 %copy-start.1 = (f32[64,16,256]{2,1,0:T(8,128)S(1)}, f32[64,16,256]{2,1,0:T(8,128)}, u32[]{:S(2)}) copy-start(f32[64,16,256]{2,1,0:T(8,128)} %accumulated.1) | copy-start | bytes 3145732
  44.7 35.6 %copy-start.2 = (s32[16,1,128]{2,1,0:T(1,128)S(1)}, s32[16,1,128]{2,1,0:T(1,128)}, u32[]{:S(2)}) copy-start(s32[16,1,128]{2,1,0:T(1,128)} %all_to_all.21) | copy-start | bytes 24580

commit v4 on v3

--- a/solution.py
+++ b/solution.py
@@ -59,19 +59,17 @@
 def stencil_products(field, parts, near, far, same_ref, cross_ref):
     for row in range(0, ROWS, 16):
         pieces = split(field[row : row + 16, :])
-        for p in range(3):
+        for p in range(2):
             parts[p, row : row + 16, :] = pieces[p]
     same = same_ref[...]
     cross = cross_ref[:HALF, :]
     down = cross_ref[HALF:, :]
     dot = functools.partial(jnp.dot, preferred_element_type=jnp.float32)
-    near[...] = dot(parts[0], same) + dot(parts[1], same) + dot(parts[2], same)
-    near[...] += dot(down, parts[0]) + dot(down, parts[1]) + dot(down, parts[2])
+    near[...] = dot(parts[0], same) + dot(parts[1], same)
+    near[...] += dot(down, parts[0]) + dot(down, parts[1])
     for side in range(0, LANES, HALF):
         cols = slice(side, side + HALF)
-        far[:, cols] = (
-            dot(parts[0, :, cols], cross) + dot(parts[1, :, cols], cross) + dot(parts[2, :, cols], cross)
-        )
+        far[:, cols] = dot(parts[0, :, cols], cross) + dot(parts[1, :, cols], cross)
 
 
 def laplacian_rows(field, near, far, row, upper):
@@ -382,7 +380,7 @@
 
     fields = (ROWS, LANES)
     whole = pltpu.VMEM(fields, jnp.float32)
-    pieces = pltpu.VMEM((3,) + fields, jnp.bfloat16)
+    pieces = pltpu.VMEM((2,) + fields, jnp.bfloat16)
     dma = pltpu.SemaphoreType.DMA
     slots_total = devices * capacity
     held = pltpu.VMEM((slots_total,) + velocity.shape[1:], jnp.float32)

time: 83.2 us -> 82.6 us (level)
  no operation moved by 1% of the time
where the time goes in v4:
time: 82.6 us; the launch traced here: 82.3 us
  blocking collectives  44.8 us (54%)
  Pallas kernels  31.3 us (38%)
  starting transfers between devices  4.03 us (5%)
  between operations  1.31 us (2%)
  waiting for transfers between devices  0.89 us (1%)
    all_to_all x1, blocking collectives, body(): lax.all_to_all(outgoing_gradient, 'shot', split_axis=0, concat_axis=0, ti...  31.6 us
    pallas_call x1, Pallas kernels, body(): pl.pallas_call(functools.partial(local_kernel, capacity, per_device), out...  21.6 us
    all_to_all x1, blocking collectives, body(): lax.all_to_all(table, 'shot', split_axis=0, concat_axis=0, tiled=True)  13.2 us
    all_to_all x1, starting transfers between devices, body(): lax.all_to_all(outgoing, 'shot', split_axis=0, concat_axis=0, tiled=True)  4.03 us
    pallas_call x1, Pallas kernels, body(): pl.pallas_call(gradient_kernel, out_shape=f32(slots_total, *velocity.shap...  3.37 us
    pallas_call x1, Pallas kernels, body(): pl.pallas_call(functools.partial(update_kernel, capacity), out_shape=(f32...  2.52 us
    pallas_call x1, Pallas kernels, body(): pl.pallas_call(functools.partial(gather_kernel, capacity), out_shape=f32(...  2.24 us
  transfers between devices with their start and end apart: 1, of which 1 were waited for; matrix products, arithmetic and copies ran while one was open for 0% of the time, Pallas kernels for 26%

profile of v4, /device:TPU:1, one launch (start us, length us, event | category | flops | bytes accessed | tf_op | source)
XLA Modules:
  0.0 82.3 jit_solution(5622419442217169894)
XLA Ops:
  0.6 1.5 %requests.1 = s32[16,128]{1,0:T(8,128)} custom-call(s32[1,32]{1,0:T(1,128)} %ids.3), custom_call_target="tpu_custom_call" | custom-call | tf_op jit(solution)/shard_map/requests/pallas_call | solution.py:371
  2.1 13.2 %all_to_all.21 = s32[16,1,128]{2,1,0:T(1,128)} all-to-all(s32[16,1,128]{2,1,0:T(1,128)} %bitcast.8), channel_id=1, replica_groups=mesh['groups'=2,'shot'=16] {'shot'}, dimensions={0} | all-to-all | bytes 16384 | tf_op jit(solution)/shard_map/all_to_all | solution.py:379
  15.3 2.2 %gather.1 = f32[64,16,256]{2,1,0:T(8,128)} custom-call(s32[16,128]{1,0:T(8,128)} %bitcast.6, f32[64,16,256]{2,1,0:T(8,128)} %velocity.3), custom_call_target="tpu_custom_call" | custom-call | tf_op jit(solution)/shard_map/gather/pallas_call | solution.py:388
  17.5 4.0 %all-to-all-start.1 = ((f32[64,16,256]{2,1,0:T(8,128)}), f32[64,16,256]{2,1,0:T(8,128)S(1)}, u32[]{:S(2)}, u32[]{:S(2)}) async-start(f32[64,16,256]{2,1,0:T(8,128)} %gather.1), calls=%async_computation.1 | async-start | bytes 2097152 | tf_op jit(solution)/shard_map/all_to_all | solution.py:397
  22.2 21.6 %local.1 = (f32[16384,512]{1,0:T(8,128)}, s32[65536,128]{1,0:T(8,128)}, bf16[32768,512]{1,0:T(8,128)(2,1)}, bf16[65536,256]{1,0:T(8,128)(2,1)}) custom-call(s32[1,8192]{1,0:T(1,128)} %cells.1, f32[2,8192]{1,0:T(2,128)} %bitcast.10, s32[1,32]{1,0:T(1,128)} %ids.3, s32[1]{0:T(128)S(6)} %copy.13.source, f32[1,2]{1,0:T(1,128)} %wavelet.1, ...), custom_call_target="tpu_custom_call" | custom-call | flops 16000000000 | bytes 4194304 | tf_op jit(solution)/shard_map/local/pallas_call | solution.py:403
  43.8 0.9 %all-to-all-done.1.arrived = f32[64,16,256]{2,1,0:T(8,128)S(1)} async-done(((f32[64,16,256]{2,1,0:T(8,128)}), f32[64,16,256]{2,1,0:T(8,128)S(1)}, u32[]{:S(2)}, u32[]{:S(2)}) %all-to-all-start.1) | async-done | bytes 1048608 | tf_op jit(solution)/shard_map/all_to_all | solution.py:397
  44.7 0.0 copy-start
  44.7 0.0 copy-start.1
  44.7 0.0 copy-start.2
  44.7 3.4 %gradient.1 = f32[64,16,256]{2,1,0:T(8,128)S(1)} custom-call(f32[64,16,256]{2,1,0:T(8,128)S(1)} %all-to-all-done.1.arrived, f32[16384,512]{1,0:T(8,128)} %get-tuple-element.6.fields_in, s32[65536,128]{1,0:T(8,128)} %get-tuple-element.7.slots_in, bf16[32768,512]{1,0:T(8,128)(2,1)} %get-tuple-element.8.same_in, bf16[65536,256]{1,0:T(8,128)(2,1)} %get-tuple-element.9.cross_in), custom_call_target="tpu_custom_call" | custom-call | tf_op jit(solution)/shard_map/gradient/pallas_call | solution.py:432
  48.1 31.6 %all_to_all.22.returned = f32[64,16,256]{2,1,0:T(8,128)S(1)} all-to-all(f32[64,16,256]{2,1,0:T(8,128)S(1)} %gradient.1), channel_id=1, replica_groups=mesh['groups'=2,'shot'=16] {'shot'}, dimensions={0} | all-to-all | bytes 2097152 | tf_op jit(solution)/shard_map/all_to_all | solution.py:444
  79.8 0.0 copy-done
  79.8 0.0 copy-done.1
  79.8 0.0 copy-done.2
  79.8 2.5 %update.1 = (f32[64,16,256]{2,1,0:T(8,128)}, f32[64,16,256]{2,1,0:T(8,128)}) custom-call(s32[16,128]{1,0:T(8,128)S(1)} %bitcast.7, f32[64,16,256]{2,1,0:T(8,128)S(1)} %all_to_all.22.returned, f32[64,16,256]{2,1,0:T(8,128)S(1)} %copy-done, f32[64,16,256]{2,1,0:T(8,128)S(1)} %copy-done.1), custom_call_target="tpu_custom_call" | custom-call | tf_op jit(solution)/shard_map/update/pallas_call | solution.py:447
Async XLA Ops:
  17.5 27.2 %all-to-all-start.1 = ((f32[64,16,256]{2,1,0:T(8,128)}), f32[64,16,256]{2,1,0:T(8,128)S(1)}, u32[]{:S(2)}, u32[]{:S(2)}) async-start(f32[64,16,256]{2,1,0:T(8,128)} %gather.1), calls=%async_computation.1 | async-start | bytes 2097152 | tf_op jit(solution)/shard_map/all_to_all | solution.py:397
  44.7 35.0 %copy-start = (f32[64,16,256]{2,1,0:T(8,128)S(1)}, f32[64,16,256]{2,1,0:T(8,128)}, u32[]{:S(2)}) copy-start(f32[64,16,256]{2,1,0:T(8,128)} %velocity.3) | copy-start | bytes 3145732
  44.7 35.0 %copy-start.1 = (f32[64,16,256]{2,1,0:T(8,128)S(1)}, f32[64,16,256]{2,1,0:T(8,128)}, u32[]{:S(2)}) copy-start(f32[64,16,256]{2,1,0:T(8,128)} %accumulated.1) | copy-start | bytes 3145732
  44.7 35.0 %copy-start.2 = (s32[16,1,128]{2,1,0:T(1,128)S(1)}, s32[16,1,128]{2,1,0:T(1,128)}, u32[]{:S(2)}) copy-start(s32[16,1,128]{2,1,0:T(1,128)} %all_to_all.21) | copy-start | bytes 24580

commit v5 on v4

--- a/solution.py
+++ b/solution.py
@@ -18,8 +18,8 @@
 ROWS = BX * AZ
 LANES = BY * TS
 HALF = TS * TS
-BLOCKS = 8
-GROUPS = 4
+BLOCKS = 4
+GROUPS = 2
 HELD = 2**16
 
 scaled_weights = (-14350.0, 8064.0, -1008.0, 128.0, -9.0)

time: 82.6 us -> 82.6 us (level)
  no operation moved by 1% of the time
where the time goes in v5:
time: 82.6 us; the launch traced here: 82.3 us
  blocking collectives  44.8 us (54%)
  Pallas kernels  31.2 us (38%)
  starting transfers between devices  4.03 us (5%)
  between operations  1.31 us (2%)
  waiting for transfers between devices  0.89 us (1%)
    all_to_all x1, blocking collectives, body(): lax.all_to_all(outgoing_gradient, 'shot', split_axis=0, concat_axis=0, ti...  31.6 us
    pallas_call x1, Pallas kernels, body(): pl.pallas_call(functools.partial(local_kernel, capacity, per_device), out...  21.6 us
    all_to_all x1, blocking collectives, body(): lax.all_to_all(table, 'shot', split_axis=0, concat_axis=0, tiled=True)  13.2 us
    all_to_all x1, starting transfers between devices, body(): lax.all_to_all(outgoing, 'shot', split_axis=0, concat_axis=0, tiled=True)  4.03 us
    pallas_call x1, Pallas kernels, body(): pl.pallas_call(gradient_kernel, out_shape=f32(slots_total, *velocity.shap...  3.37 us
    pallas_call x1, Pallas kernels, body(): pl.pallas_call(functools.partial(update_kernel, capacity), out_shape=(f32...  2.49 us
    pallas_call x1, Pallas kernels, body(): pl.pallas_call(functools.partial(gather_kernel, capacity), out_shape=f32(...  2.24 us
  transfers between devices with their start and end apart: 1, of which 1 were waited for; matrix products, arithmetic and copies ran while one was open for 0% of the time, Pallas kernels for 26%

profile of v5, /device:TPU:1, one launch (start us, length us, event | category | flops | bytes accessed | tf_op | source)
XLA Modules:
  0.0 82.3 jit_solution(494650757050989459)
XLA Ops:
  0.6 1.5 %requests.1 = s32[16,128]{1,0:T(8,128)} custom-call(s32[1,32]{1,0:T(1,128)} %ids.3), custom_call_target="tpu_custom_call" | custom-call | tf_op jit(solution)/shard_map/requests/pallas_call | solution.py:371
  2.1 13.2 %all_to_all.21 = s32[16,1,128]{2,1,0:T(1,128)} all-to-all(s32[16,1,128]{2,1,0:T(1,128)} %bitcast.8), channel_id=1, replica_groups=mesh['groups'=2,'shot'=16] {'shot'}, dimensions={0} | all-to-all | bytes 16384 | tf_op jit(solution)/shard_map/all_to_all | solution.py:379
  15.3 2.2 %gather.1 = f32[64,16,256]{2,1,0:T(8,128)} custom-call(s32[16,128]{1,0:T(8,128)} %bitcast.6, f32[64,16,256]{2,1,0:T(8,128)} %velocity.3), custom_call_target="tpu_custom_call" | custom-call | tf_op jit(solution)/shard_map/gather/pallas_call | solution.py:388
  17.5 4.0 %all-to-all-start.1 = ((f32[64,16,256]{2,1,0:T(8,128)}), f32[64,16,256]{2,1,0:T(8,128)S(1)}, u32[]{:S(2)}, u32[]{:S(2)}) async-start(f32[64,16,256]{2,1,0:T(8,128)} %gather.1), calls=%async_computation.1 | async-start | bytes 2097152 | tf_op jit(solution)/shard_map/all_to_all | solution.py:397
  22.2 21.6 %local.1 = (f32[16384,512]{1,0:T(8,128)}, s32[65536,128]{1,0:T(8,128)}, bf16[32768,512]{1,0:T(8,128)(2,1)}, bf16[65536,256]{1,0:T(8,128)(2,1)}) custom-call(s32[1,8192]{1,0:T(1,128)} %cells.1, f32[2,8192]{1,0:T(2,128)} %bitcast.10, s32[1,32]{1,0:T(1,128)} %ids.3, s32[1]{0:T(128)S(6)} %copy.13.source, f32[1,2]{1,0:T(1,128)} %wavelet.1, ...), custom_call_target="tpu_custom_call" | custom-call | flops 16000000000 | bytes 4194304 | tf_op jit(solution)/shard_map/local/pallas_call | solution.py:403
  43.8 0.9 %all-to-all-done.1.arrived = f32[64,16,256]{2,1,0:T(8,128)S(1)} async-done(((f32[64,16,256]{2,1,0:T(8,128)}), f32[64,16,256]{2,1,0:T(8,128)S(1)}, u32[]{:S(2)}, u32[]{:S(2)}) %all-to-all-start.1) | async-done | bytes 1048608 | tf_op jit(solution)/shard_map/all_to_all | solution.py:397
  44.7 0.0 copy-start
  44.7 0.0 copy-start.1
  44.7 0.0 copy-start.2
  44.7 3.4 %gradient.1 = f32[64,16,256]{2,1,0:T(8,128)S(1)} custom-call(f32[64,16,256]{2,1,0:T(8,128)S(1)} %all-to-all-done.1.arrived, f32[16384,512]{1,0:T(8,128)} %get-tuple-element.6.fields_in, s32[65536,128]{1,0:T(8,128)} %get-tuple-element.7.slots_in, bf16[32768,512]{1,0:T(8,128)(2,1)} %get-tuple-element.8.same_in, bf16[65536,256]{1,0:T(8,128)(2,1)} %get-tuple-element.9.cross_in), custom_call_target="tpu_custom_call" | custom-call | tf_op jit(solution)/shard_map/gradient/pallas_call | solution.py:432
  48.1 31.6 %all_to_all.22.returned = f32[64,16,256]{2,1,0:T(8,128)S(1)} all-to-all(f32[64,16,256]{2,1,0:T(8,128)S(1)} %gradient.1), channel_id=1, replica_groups=mesh['groups'=2,'shot'=16] {'shot'}, dimensions={0} | all-to-all | bytes 2097152 | tf_op jit(solution)/shard_map/all_to_all | solution.py:444
  79.8 0.0 copy-done
  79.8 0.0 copy-done.1
  79.8 0.0 copy-done.2
  79.8 2.5 %update.1 = (f32[64,16,256]{2,1,0:T(8,128)}, f32[64,16,256]{2,1,0:T(8,128)}) custom-call(s32[16,128]{1,0:T(8,128)S(1)} %bitcast.7, f32[64,16,256]{2,1,0:T(8,128)S(1)} %all_to_all.22.returned, f32[64,16,256]{2,1,0:T(8,128)S(1)} %copy-done, f32[64,16,256]{2,1,0:T(8,128)S(1)} %copy-done.1), custom_call_target="tpu_custom_call" | custom-call | tf_op jit(solution)/shard_map/update/pallas_call | solution.py:447
Async XLA Ops:
  17.5 27.2 %all-to-all-start.1 = ((f32[64,16,256]{2,1,0:T(8,128)}), f32[64,16,256]{2,1,0:T(8,128)S(1)}, u32[]{:S(2)}, u32[]{:S(2)}) async-start(f32[64,16,256]{2,1,0:T(8,128)} %gather.1), calls=%async_computation.1 | async-start | bytes 2097152 | tf_op jit(solution)/shard_map/all_to_all | solution.py:397
  44.7 35.0 %copy-start = (f32[64,16,256]{2,1,0:T(8,128)S(1)}, f32[64,16,256]{2,1,0:T(8,128)}, u32[]{:S(2)}) copy-start(f32[64,16,256]{2,1,0:T(8,128)} %velocity.3) | copy-start | bytes 3145732
  44.7 35.0 %copy-start.1 = (f32[64,16,256]{2,1,0:T(8,128)S(1)}, f32[64,16,256]{2,1,0:T(8,128)}, u32[]{:S(2)}) copy-start(f32[64,16,256]{2,1,0:T(8,128)} %accumulated.1) | copy-start | bytes 3145732
  44.7 35.0 %copy-start.2 = (s32[16,1,128]{2,1,0:T(1,128)S(1)}, s32[16,1,128]{2,1,0:T(1,128)}, u32[]{:S(2)}) copy-start(s32[16,1,128]{2,1,0:T(1,128)} %all_to_all.21) | copy-start | bytes 24580
